TPU v7x, 32 devices: a whole 2x2x4 slice. The times are simulated.
32 devices in a mesh: tiles: 2 (over y), strip: 4 (over z), col: 2 (over x), expo: 2 (over core).
Axes of the slice: x: 2, y: 2, z: 4, core: 2. Of those that a mesh axis runs over, the one named last changes fastest.
Arguments:
- mask_params: float32 [2, 2048, 256], P('expo', ('tiles', 'strip'), 'col'), parts along dimension 1, may hold values from -3 to 3
- target: int32 [2048, 256], P(('tiles', 'strip'), 'col'), parts along dimension 0, may hold values from 0 to 1, as said below
- col_taps: bfloat16 [24, 2, 65], replicated, may hold values from -0.75 to 0.75
- row_taps: bfloat16 [24, 2, 65], replicated, may hold values from -0.75 to 0.75
- kernel_weights: float32 [24], replicated, may hold values from 0.05 to 0.5
Outputs:
- new_params: float32 [2, 2048, 256], P('expo', ('tiles', 'strip'), 'col'), parts along dimension 1
- resist: float32 [2048, 256], P(('tiles', 'strip'), 'col'), parts along dimension 0
- mean_loss: float32 [2], P('tiles'), parts along dimension 0
There are 2 independent parts, one for each index of `tiles`. A program takes and returns all parts, laid end to end along the dimension named above; an argument that names none is the same for every part. Nothing has to cross between parts.
Inputs may be any that keep to these rules, and one draw needn't show every extreme that they name: `target`: 1 where the layout is printed, 0 elsewhere.
All inputs are finite; a program needn't handle non-finite values.
Results may differ from a plain program's by a relative error of at most 0.0078.
Values may be sent and summed in bfloat16 or wider, within the bound.
A program may use at most 64 MiB of HBM per device.

v0:
```python
import jax
import jax.numpy as jnp
from jax import lax
from jax.sharding import PartitionSpec as P

HALF = 32


mask_slope = 4.0
resist_steep = 4.0
resist_level = 3.0
step_length = 0.5
norm_eps = 1e-06


def extended(array, sides, width):
    for axis, dim in sides:
        peers, length = (lax.axis_size(axis), array.shape[dim])
        up = [(i, (i + 1) % peers) for i in range(peers - 1)]
        down = [(j, i) for i, j in up]
        last = lax.slice_in_dim(array, length - width, length, axis=dim)
        first = lax.slice_in_dim(array, 0, width, axis=dim)
        before = lax.ppermute(last, axis, up)
        after = lax.ppermute(first, axis, down)
        array = jnp.concatenate([before, array, after], axis=dim)
    return array


def block_size():
    return 128


def toeplitz(tap_values, block_len):
    tap_count = tap_values.shape[-1]
    window_len = block_len + tap_count - 1
    padded_taps = jnp.concatenate(
        [tap_values, jnp.zeros(tap_values.shape[:-1] + (block_len,), tap_values.dtype)], axis=-1
    )
    repeated = jnp.tile(padded_taps, (1,) * (tap_values.ndim - 1) + (block_len,))
    return repeated[..., : block_len * window_len].reshape(
        tap_values.shape[:-1] + (block_len, window_len)
    )


def col_pass(source, tap_table):
    block_len, window_len = (tap_table.shape[1], tap_table.shape[2])
    length = source.shape[-1] - window_len + block_len
    windows = jnp.stack([source], axis=1)
    result = jnp.einsum("rnw,pow->prno", windows, tap_table, preferred_element_type=jnp.float32)
    return result.reshape(tap_table.shape[0], source.shape[0], length)


def row_pass(source, tap_table):
    block_len, window_len = (tap_table.shape[1], tap_table.shape[2])
    length = source.shape[1] - window_len + block_len
    windows = jnp.stack(
        [
            source[:, offset * block_len : offset * block_len + window_len, :]
            for offset in range(length // block_len)
        ],
        axis=1,
    )
    result = jnp.einsum("pnwc,qow->pqnoc", windows, tap_table, preferred_element_type=jnp.float32)
    return result.reshape(source.shape[0], tap_table.shape[0], length, source.shape[2])


def col_adjoint(source, tap_table):
    block_len, window_len = (tap_table.shape[1], tap_table.shape[2])
    length = source.shape[-1] - window_len + block_len
    windows = jnp.stack([source], axis=2)
    result = jnp.einsum("prnw,pow->rno", windows, tap_table, preferred_element_type=jnp.float32)
    return result.reshape(source.shape[1], length)


def shards(mask_params, target, col_taps, row_taps, kernel_weights):
    row_count, col_count = target.shape
    mask_field = jax.nn.sigmoid(mask_slope * mask_params[0])
    mask_half = mask_field.astype(jnp.bfloat16)
    col_block = block_size()
    row_block = block_size()
    mask_ext = extended(mask_half, (("strip", 0), ("col", 1)), HALF)

    def add_intensity(running, kernel):
        col_pair = col_taps[kernel]
        row_pair = row_taps[kernel]
        columns = col_pass(mask_ext, toeplitz(col_pair, col_block)).astype(jnp.bfloat16)
        pair_sums = row_pass(columns, toeplitz(row_pair, row_block))
        real_part = pair_sums[0, 0] - pair_sums[1, 1]
        imag_part = pair_sums[0, 1] + pair_sums[1, 0]
        updated = running + kernel_weights[kernel] * (real_part * real_part + imag_part * imag_part)
        return (updated, (real_part, imag_part))

    kernel_ids = jnp.arange(kernel_weights.shape[0], dtype=jnp.int32)
    zero_field = jnp.zeros((row_count, col_count), jnp.float32)
    intensity, stored = lax.scan(add_intensity, zero_field, kernel_ids)
    summed = lax.psum(intensity, "expo")
    resist = jax.nn.sigmoid(resist_steep * (summed - resist_level))
    mismatch = resist - target.astype(jnp.float32)
    pixels = row_count * col_count * lax.axis_size("strip") * lax.axis_size("col")
    loss_local = jnp.sum(mismatch * mismatch)
    loss_sum = lax.psum(loss_local, ("strip", "col"))
    slope_field = 2.0 * mismatch * resist_steep * resist * (1.0 - resist)

    def add_gradient(running, inputs):
        kernel, real_part, imag_part = inputs
        col_pair = col_taps[kernel]
        row_pair = row_taps[kernel]
        weighting = 2.0 * kernel_weights[kernel] * slope_field
        products = jnp.stack([weighting * real_part, weighting * imag_part]).astype(jnp.bfloat16)
        product_ext = extended(products, (("strip", 1),), HALF)
        returned = row_pass(product_ext, toeplitz(row_pair[:, ::-1], row_block))
        unrolled = jnp.stack(
            [returned[0, 0] + returned[1, 1], returned[1, 0] - returned[0, 1]]
        ).astype(jnp.bfloat16)
        unrolled_ext = extended(unrolled, (("col", 2),), HALF)
        return (running + col_adjoint(unrolled_ext, toeplitz(col_pair[:, ::-1], col_block)), None)

    descent, unused = lax.scan(add_gradient, zero_field, (kernel_ids, stored[0], stored[1]))
    gradient = descent * mask_slope * mask_field * (1.0 - mask_field)
    grad_squares = jnp.sum(gradient * gradient)
    square_sum = lax.psum(grad_squares, ("strip", "col", "expo"))
    root_mean = jnp.sqrt(square_sum / (lax.axis_size("expo") * pixels) + norm_eps)
    new_params = mask_params - step_length * gradient[None] / root_mean
    mean_loss = (loss_sum / pixels).reshape(1)
    return (new_params, resist, mean_loss)


def solution(mesh):
    return jax.shard_map(
        shards,
        mesh=mesh,
        in_specs=(
            P("expo", ("tiles", "strip"), "col"),
            P(("tiles", "strip"), "col"),
            P(),
            P(),
            P(),
        ),
        out_specs=(P("expo", ("tiles", "strip"), "col"), P(("tiles", "strip"), "col"), P("tiles")),
        check_vma=False,
    )
```

profile of v0, /device:TPU:0, one launch (start us, length us, event | category | flops | bytes accessed | tf_op | source)
XLA Modules:
  0.0 801.5 jit_solution(15718260283883890776)
XLA Ops:
  8.2 4.9 collective-permute-start.4
  14.5 4.2 collective-permute-done.5
  24.2 4.3 collective-permute-done.7
  28.8 172.5 %while.26 = (s32[]{:T(128)}, f32[256,128]{1,0:T(8,128)S(1)}, f32[24,256,128]{2,1,0:T(8,128)}, f32[24,256,128]{2,1,0:T(8,128)}, s32[24]{0:T(128)S(1)}, /*index=5*...) while((s32[]{:T(128)}, f32[256,128]{1,0:T(8,128)S(1)}, ...), condition=%wide.region_1.2_spmd.clone, body=%wide.region_0.1_spmd.clone.sunk | while | flops 82296832 | bytes 4555409 | solution.py:95
  202.0 17.4 %all-reduce.6.cloned.1.call-done = f32[256,128]{1,0:T(8,128)} async-done(((f32[256,128]{1,0:T(8,128)}), f32[256,128]{1,0:T(8,128)}) %all-reduce.6.cloned.1.call-update) | async-done | bytes 131088 | tf_op jit(solution)/shard_map/psum | solution.py:96
  221.7 521.3 %while.27 = (s32[]{:T(128)}, f32[256,128]{1,0:T(8,128)S(1)}, s32[24]{0:T(128)S(1)}, bf16[24,2,65]{2,1,0:T(2,128)(2,1)}, f32[24]{0:T(128)}, /*index=5*/f32[256,12...) while((s32[]{:T(128)}, f32[256,128]{1,0:T(8,128)S(1)}, ...), condition=%wide.region_4.5_spmd.clone, body=%wide.region_3.4_spmd.clone.sunk | while | flops 77824000 | bytes 7152573 | solution.py:118
  238.5 4.5 collective-permute-start.3
  261.5 4.5 collective-permute-start.3
  284.5 4.5 collective-permute-start.3
  306.0 4.5 collective-permute-start.3
  327.5 4.5 collective-permute-start.3
  349.0 4.5 collective-permute-start.3
  370.5 4.5 collective-permute-start.3
  392.0 4.5 collective-permute-start.3
  413.5 4.5 collective-permute-start.3
  435.0 4.5 collective-permute-start.3
  456.6 4.5 collective-permute-start.3
  478.2 4.5 collective-permute-start.3
  499.7 4.5 collective-permute-start.3
  521.2 4.5 collective-permute-start.3
  542.7 4.5 collective-permute-start.3
  564.3 4.5 collective-permute-start.3
  585.8 4.5 collective-permute-start.3
  607.3 4.5 collective-permute-start.3
  628.8 4.5 collective-permute-start.3
  650.3 4.5 collective-permute-start.3
  672.0 4.5 collective-permute-start.3
  693.5 4.5 collective-permute-start.3
  715.0 4.5 collective-permute-start.3
  736.5 4.5 collective-permute-start.3
  743.6 30.1 %psum.22 = f32[]{:T(128)} all-reduce(f32[]{:T(128)} %multiply_reduce_fusion.1), channel_id=1, replica_groups=mesh['tiles'=2,'strip'=4,'col'=2,'expo'=2] {'strip','col','expo'}, use_global_device_ids=true, to_apply=%region_6.7 | all-reduce | flops 1 | bytes 8 | tf_op jit(solution)/shard_map/psum | solution.py:121
  775.2 17.7 %psum.23 = f32[]{:T(128)} all-reduce(f32[]{:T(128)} %get-tuple-element.217), channel_id=1, replica_groups=mesh['tiles'=2,'strip'=4,'col'=2,'expo'=2] {'strip','col'}, use_global_device_ids=true, to_apply=%region_8.9 | all-reduce | flops 1 | bytes 8 | tf_op jit(solution)/shard_map/psum | solution.py:101
  (1351 shorter events, 481.2 us)
Async XLA Ops:
  7.2 212.2 %all-reduce.6.cloned.1.call-start = ((), (), s32[]{:S(2)}) async-start(), calls=%async_computation | async-start | bytes 262144 | tf_op jit(solution)/shard_map/psum | solution.py:96
  8.2 6.3 collective-permute-start.4
  22.2 6.3 collective-permute-start.7
  227.1 6.4 collective-permute-start
  237.2 6.6 collective-permute-start.2
  238.5 6.1 collective-permute-start.3
  250.4 6.2 collective-permute-start
  260.2 6.6 collective-permute-start.2
  261.5 6.1 collective-permute-start.3
  273.4 6.2 collective-permute-start
  283.2 6.6 collective-permute-start.2
  304.7 6.6 collective-permute-start.2
  326.2 6.6 collective-permute-start.2
  347.7 6.6 collective-permute-start.2
  369.2 6.6 collective-permute-start.2
  390.7 6.6 collective-permute-start.2
  412.2 6.6 collective-permute-start.2
  433.7 6.6 collective-permute-start.2
  455.3 6.6 collective-permute-start.2
  476.9 6.6 collective-permute-start.2
  498.4 6.6 collective-permute-start.2
  519.9 6.6 collective-permute-start.2
  541.4 6.6 collective-permute-start.2
  563.0 6.6 collective-permute-start.2
  584.5 6.6 collective-permute-start.2
  606.0 6.6 collective-permute-start.2
  627.5 6.6 collective-permute-start.2
  649.0 6.6 collective-permute-start.2
  670.7 6.6 collective-permute-start.2
  692.2 6.6 collective-permute-start.2
  713.7 6.6 collective-permute-start.2
  735.2 6.6 collective-permute-start.2
  (97 other events, 1233.9 us)
Sparse Core Ops, SparseCore 0:
  202.1 17.2 all-reduce.5
where the time goes:
time: 807 us; the launch traced here: 802 us
  starting transfers between devices  233 us (29%)
  local copies, waits for them, and re-layouts  185 us (23%)
  loops' own time  116 us (14%)
  waiting for transfers between devices  114 us (14%)
  other arithmetic  65.4 us (8%)
  blocking collectives  47.8 us (6%)
  matrix products  23.3 us (3%)
  between operations  16.7 us (2%)
    ppermute x50, starting transfers between devices, extended(): before = lax.ppermute(last, axis, up)  169 us
    ppermute x50, waiting for transfers between devices, extended(): after = lax.ppermute(first, axis, down)  77.3 us
    another operation x1, loops' own time, shards(): lax.scan(add_gradient, zero_field, (kernel_ids, stored[0], stored[1]))  67 us
    ppermute x50, starting transfers between devices, extended(): after = lax.ppermute(first, axis, down)  64.6 us
    another operation x1, loops' own time, shards(): intensity, stored = lax.scan(add_intensity, zero_field, kernel_ids)  48.9 us
    another operation x192, local copies, waits for them, and re-layouts, toeplitz(): jnp.tile(padded_taps, (1,) * (tap_values.ndim - 1) + (block_len,))  42.5 us
    psum x1, blocking collectives, shards(): square_sum = lax.psum(grad_squares, ('strip', 'col', 'expo'))  30.1 us
    dynamic_slice x24, local copies, waits for them, and re-layouts, add_gradient(): weighting = 2.0 * kernel_weights[kernel] * slope_field  29.8 us
  transfers between devices with their start and end apart: 101, of which 52 were waited for; matrix products, arithmetic and copies ran while one was open for 7% of the time, Pallas kernels for 0%

commit v1 on v0

v1 whole, which is shorter than its diff:
```python
import functools

import jax
import jax.numpy as jnp
from jax import lax
from jax.experimental import pallas as pl
from jax.experimental.pallas import tpu as pltpu
from jax.sharding import PartitionSpec as P

mask_slope = 4.0
resist_steep = 4.0
resist_level = 3.0
step_length = 0.5
norm_eps = 1e-06

MESH = pl.DeviceIdType.MESH
F32 = jnp.float32
BF16 = jnp.bfloat16
WINDOW = 256
DIRECTIONS = [(a, b) for a in (-1, 0, 1) for b in (-1, 0, 1) if (a, b) != (0, 0)]


def blocks_of(total_out, reach):
    most = WINDOW - reach
    count = -(-total_out // most)
    size = -(-total_out // (count * 16)) * 16
    found = []
    for start in range(0, total_out, size):
        rows = min(size, total_out - start)
        window = min(start, total_out + reach - WINDOW)
        found.append((start, rows, window, start - window))
    return found


def dot(a, b):
    return jnp.dot(a, b, preferred_element_type=F32)


def dot_t(a, b):
    return lax.dot_general(a, b, (((1,), (1,)), ((), ())), preferred_element_type=F32)


def body(
    sizes,
    params_ref,
    target_ref,
    vec_ref,
    weight_ref,
    new_ref,
    resist_ref,
    loss_ref,
    halo,
    ext,
    col_mats,
    fwd_mats,
    adj_mats,
    columns,
    fields,
    intensity,
    other,
    slope,
    descent,
    partial,
    slots,
    halo_send,
    halo_recv,
    expo_send,
    expo_recv,
    sum_send,
    sum_recv,
):
    strips, cols, expos, half = sizes
    kernels = vec_ref.shape[0]
    rows, width = target_ref.shape
    two = 2 * half
    wide = width + 2 * two
    group = strips * cols * expos
    strip, col, expo = (lax.axis_index("strip"), lax.axis_index("col"), lax.axis_index("expo"))
    me = (strip * cols + col) * expos + expo

    def device(index):
        return {
            "strip": index // (cols * expos),
            "col": (index // expos) % cols,
            "expo": index % expos,
        }

    halo[...] = jnp.zeros_like(halo)

    barrier = pltpu.get_barrier_semaphore()

    def greet(step, carry):
        pl.semaphore_signal(
            barrier, inc=1, device_id=device(lax.rem(me + step, group)), device_id_type=MESH
        )
        return carry

    lax.fori_loop(1, group, greet, 0)

    mask = jax.nn.sigmoid(mask_slope * params_ref[0])
    halo[0, two : two + rows, width : 2 * width] = mask.astype(BF16)
    halo[1, two : two + rows, width : 2 * width] = target_ref[...].astype(F32).astype(BF16)

    def transfer(number):
        down, right = DIRECTIONS[number]
        source = {-1: (two, two), 0: (two, rows), 1: (rows, two)}[down]
        landing = {-1: two + rows, 0: two, 1: 0}[down]
        lane = {-1: 2 * width, 0: width, 1: 0}[right]
        return pltpu.make_async_remote_copy(
            src_ref=halo.at[:, pl.ds(source[0], source[1]), pl.ds(width, width)],
            dst_ref=halo.at[:, pl.ds(landing, source[1]), pl.ds(lane, width)],
            send_sem=halo_send.at[number],
            recv_sem=halo_recv.at[number],
            device_id={
                "strip": jnp.clip(strip + down, 0, strips - 1),
                "col": jnp.clip(col + right, 0, cols - 1),
            },
            device_id_type=MESH,
        )

    def inside(down, right):
        to_strip, to_col = (strip + down, col + right)
        return (to_strip >= 0) & (to_strip < strips) & (to_col >= 0) & (to_col < cols)

    pl.semaphore_wait(barrier, group - 1)

    for number, (down, right) in enumerate(DIRECTIONS):

        @pl.when(inside(down, right))
        def _():
            transfer(number).start()

    def spread(k, row, count):
        line = vec_ref[k, row : row + 1, :]
        return pltpu.roll(
            jnp.broadcast_to(line, (count, line.shape[1])), 0, 1, stride=1, stride_axis=0
        )

    span = fwd_mats.shape[2]

    def build(k, carry):
        for part in range(2):
            col_mats[k, part] = spread(k, part, wide).astype(BF16)
        t0, t1 = (spread(k, 2, span), spread(k, 3, span))
        fwd_mats[k, 0, :, :WINDOW] = t0.astype(BF16)
        fwd_mats[k, 0, :, WINDOW:] = (-t1).astype(BF16)
        fwd_mats[k, 1, :, :WINDOW] = t1.astype(BF16)
        fwd_mats[k, 1, :, WINDOW:] = t0.astype(BF16)
        g0, g1 = (spread(k, 4, span), spread(k, 5, span))
        adj_mats[k, 0, :, :WINDOW] = g0.astype(BF16)
        adj_mats[k, 0, :, WINDOW:] = g1.astype(BF16)
        adj_mats[k, 1, :, :WINDOW] = (-g1).astype(BF16)
        adj_mats[k, 1, :, WINDOW:] = g0.astype(BF16)
        return carry

    lax.fori_loop(0, kernels, build, 0)
    intensity[...] = jnp.zeros_like(intensity)
    descent[...] = jnp.zeros_like(descent)

    for number, (down, right) in enumerate(DIRECTIONS):

        @pl.when(inside(down, right))
        def _():
            transfer(number).wait_send()

        @pl.when(inside(-down, -right))
        def _():
            transfer(number).wait_recv()

    lanes = halo.shape[2]
    shifted = pltpu.roll(halo[0].astype(F32), lanes - (width - two), 1)
    ext[...] = shifted[:, :wide].astype(BF16)

    def forward(k, carry):
        for part in range(2):
            columns[part] = dot(ext[...], col_mats[k, part]).astype(BF16)
        weight = weight_ref[k]
        for start, count, window, offset in blocks_of(rows + two, two):
            source = jnp.concatenate(
                [columns[0, window : window + WINDOW, :], columns[1, window : window + WINDOW, :]],
                axis=0,
            )
            real_part = dot(fwd_mats[k, 0, offset : offset + count, :], source)
            imag_part = dot(fwd_mats[k, 1, offset : offset + count, :], source)
            fields[k, 0, start : start + count, :] = real_part
            fields[k, 1, start : start + count, :] = imag_part
            intensity[start : start + count, :] += weight * (
                real_part * real_part + imag_part * imag_part
            )
        return carry

    lax.fori_loop(0, kernels, forward, 0)

    swap = pltpu.make_async_remote_copy(
        src_ref=intensity,
        dst_ref=other,
        send_sem=expo_send,
        recv_sem=expo_recv,
        device_id={"expo": 1 - expo},
        device_id_type=MESH,
    )
    swap.start()
    swap.wait()

    tall = rows + two
    resist = jax.nn.sigmoid(resist_steep * (intensity[...] + other[...] - resist_level))
    target_ext = pltpu.roll(
        halo[1, half : half + tall, :].astype(F32), lanes - (width - half), 1
    )[:, :wide]
    row_ids = lax.broadcasted_iota(jnp.int32, (tall, wide), 0) + (strip * rows - half)
    lane_ids = lax.broadcasted_iota(jnp.int32, (tall, wide), 1)
    col_ids = lane_ids + (col * width - half)
    kept = (
        (row_ids >= 0)
        & (row_ids < strips * rows)
        & (col_ids >= 0)
        & (col_ids < cols * width)
        & (lane_ids < width + two)
    )
    mismatch = resist - target_ext
    slope[...] = jnp.where(kept, 2.0 * mismatch * resist_steep * resist * (1.0 - resist), 0.0)
    own = pltpu.roll(resist[half : half + rows, :], wide - half, 1)[:, :width]
    resist_ref[...] = own
    own_miss = own - target_ref[...].astype(F32)
    loss_line = jnp.sum(own_miss * own_miss, axis=0, keepdims=True)

    def backward(k, carry):
        weighting = (2.0 * weight_ref[k]) * slope[...]
        products = [(weighting * fields[k, part]).astype(BF16) for part in range(2)]
        taps = jnp.concatenate(
            [col_mats[k, part, two : two + width, :] for part in range(2)], axis=1
        )
        for start, count, window, offset in blocks_of(rows, two):
            source = jnp.concatenate(
                [products[part][window : window + WINDOW, :] for part in range(2)], axis=0
            )
            returned = jnp.concatenate(
                [
                    dot(adj_mats[k, part, offset : offset + count, :], source).astype(BF16)
                    for part in range(2)
                ],
                axis=1,
            )
            descent[start : start + count, :] += dot_t(returned, taps)
        return carry

    lax.fori_loop(0, kernels, backward, 0)

    mask = jax.nn.sigmoid(mask_slope * params_ref[0])
    gradient = descent[...] * mask_slope * mask * (1.0 - mask)
    descent[...] = gradient
    square_line = jnp.sum(gradient * gradient, axis=0, keepdims=True)
    which = lax.broadcasted_iota(jnp.int32, partial.shape, 0)
    sums = jnp.where(which == 0, loss_line, jnp.where(which == 1, square_line, 0.0))
    partial[...] = sums
    slots[me] = sums

    def share(step):
        return pltpu.make_async_remote_copy(
            src_ref=partial,
            dst_ref=slots.at[me],
            send_sem=sum_send.at[step],
            recv_sem=sum_recv.at[me],
            device_id=device(lax.rem(me + step, group)),
            device_id_type=MESH,
        )

    def arrival(step):
        source = lax.rem(me + step, group)
        return pltpu.make_async_remote_copy(
            src_ref=partial,
            dst_ref=slots.at[source],
            send_sem=sum_send.at[step],
            recv_sem=sum_recv.at[source],
            device_id=device(source),
            device_id_type=MESH,
        )

    def send_sums(step, carry):
        share(step).start()
        return carry

    def wait_sums(step, carry):
        arrival(step).wait()
        return carry

    lax.fori_loop(1, group, send_sums, 0)
    lax.fori_loop(1, group, wait_sums, 0)

    total = jnp.sum(slots[...], axis=0)
    pixels = rows * width * strips * cols
    loss_ref[0] = jnp.sum(total[0:1, :]) / (expos * pixels)
    square_sum = jnp.sum(total[1:2, :], axis=1, keepdims=True)
    root_mean = jnp.sqrt(square_sum / (expos * pixels) + norm_eps)
    new_ref[0] = params_ref[0] - step_length * descent[...] / root_mean


def tap_lines(col_taps, row_taps, length):
    kernels, parts, taps = col_taps.shape
    col, row = (col_taps.astype(F32), row_taps.astype(F32))
    gap = jnp.zeros((kernels, parts, length - taps), F32)
    wrap = jnp.concatenate([col[..., :1], gap, col[..., :0:-1]], axis=-1)
    ahead = jnp.concatenate([row, gap], axis=-1)
    turned = jnp.concatenate([row[..., ::-1], gap], axis=-1)
    return jnp.concatenate([wrap, ahead, turned, jnp.zeros_like(wrap)], axis=1)


def shards(mask_params, target, col_taps, row_taps, kernel_weights):
    rows, width = target.shape
    kernels, _, taps = col_taps.shape
    half = taps // 2
    two = 2 * half
    wide, tall = (width + 2 * two, rows + two)
    strips, cols, expos = (lax.axis_size(a) for a in ("strip", "col", "expo"))
    group = strips * cols * expos
    span = WINDOW - two
    vmem = pl.BlockSpec(memory_space=pltpu.VMEM)
    smem = pl.BlockSpec(memory_space=pltpu.SMEM)
    dma = pltpu.SemaphoreType.DMA
    return pl.pallas_call(
        functools.partial(body, (strips, cols, expos, half)),
        out_shape=(
            jax.ShapeDtypeStruct(mask_params.shape, F32),
            jax.ShapeDtypeStruct(target.shape, F32),
            jax.ShapeDtypeStruct((1,), F32),
        ),
        in_specs=[vmem, vmem, vmem, smem],
        out_specs=(vmem, vmem, smem),
        scratch_shapes=[
            pltpu.VMEM((2, rows + 2 * two, 3 * width), BF16),
            pltpu.VMEM((rows + 2 * two, wide), BF16),
            pltpu.VMEM((kernels, 2, wide, wide), BF16),
            pltpu.VMEM((kernels, 2, span, 2 * WINDOW), BF16),
            pltpu.VMEM((kernels, 2, span, 2 * WINDOW), BF16),
            pltpu.VMEM((2, rows + 2 * two, wide), BF16),
            pltpu.VMEM((kernels, 2, tall, wide), F32),
            pltpu.VMEM((tall, wide), F32),
            pltpu.VMEM((tall, wide), F32),
            pltpu.VMEM((tall, wide), F32),
            pltpu.VMEM((rows, width), F32),
            pltpu.VMEM((8, width), F32),
            pltpu.VMEM((group, 8, width), F32),
            dma((8,)),
            dma((8,)),
            dma,
            dma,
            dma((group,)),
            dma((group,)),
        ],
        compiler_params=pltpu.CompilerParams(
            collective_id=0, has_side_effects=True, vmem_limit_bytes=56 * 1024 * 1024
        ),
    )(mask_params, target, tap_lines(col_taps, row_taps, wide), kernel_weights)


def solution(mesh):
    return jax.shard_map(
        shards,
        mesh=mesh,
        in_specs=(
            P("expo", ("tiles", "strip"), "col"),
            P(("tiles", "strip"), "col"),
            P(),
            P(),
            P(),
        ),
        out_specs=(P("expo", ("tiles", "strip"), "col"), P(("tiles", "strip"), "col"), P("tiles")),
        check_vma=False,
    )
```

time: 807 us -> 54.2 us (0.07)
  starting transfers between devices: 233 us -> 0 us
  local copies, waits for them, and re-layouts: 185 us -> 3.97 us
  loops' own time: 116 us -> 0 us
  waiting for transfers between devices: 114 us -> 0 us
  other arithmetic: 65.4 us -> 0.8 us
  blocking collectives: 47.8 us -> 0 us
  Pallas kernels: 0 us -> 46.5 us
  matrix products: 23.3 us -> 0 us
  between operations: 16.7 us -> 2.53 us
    ppermute x100 -> x0, starting transfers between devices: 233 us -> none  [the longest x50 169 us: extended(): before = lax.ppermute(last, axis, up)]
    another operation x2 -> x0, loops' own time: 116 us -> none  [the longest x1 67 us: shards(): lax.scan(add_gradient, zero_field, (kernel_ids, stored[0], stored[1]))]
    ppermute x100 -> x0, waiting for transfers between devices: 96.9 us -> none  [the longest x50 77.3 us: extended(): after = lax.ppermute(first, axis, down)]
    dynamic_slice x96 -> x0, local copies, waits for them, and re-layouts: 72 us -> none  [the longest x24 29.8 us: add_gradient(): weighting = 2.0 * kernel_weights[kernel] * slope_field]
    psum x2 -> x0, blocking collectives: 47.8 us -> none  [the longest x1 30.1 us: shards(): square_sum = lax.psum(grad_squares, ('strip', 'col', 'expo'))]
    pallas_call x0 -> x1, Pallas kernels: none -> 46.5 us  [shards(): pl.pallas_call(functools.partial(body, (strips, cols, expos, half)), out_...]
    another operation x216 -> x0, local copies, waits for them, and re-layouts: 43 us -> none  [the longest x192 42.5 us: toeplitz(): jnp.tile(padded_taps, (1,) * (tap_values.ndim - 1) + (block_len,))]
    squeeze x48 -> x0, local copies, waits for them, and re-layouts: 32.7 us -> none  [the longest x24 16.4 us: add_gradient(): row_pair = row_taps[kernel]]
  transfers between devices with their start and end apart: 101 -> 0, of which waited for: 52 -> 0; matrix products, arithmetic and copies ran while one was open for 7% -> 0% of each run, Pallas kernels for 0% -> 0%
where the time goes in v1:
time: 54.2 us; the launch traced here: 53.8 us
  Pallas kernels  46.5 us (86%)
  local copies, waits for them, and re-layouts  3.97 us (7%)
  between operations  2.53 us (5%)
  other arithmetic  0.8 us (1%)
    pallas_call x1, Pallas kernels, shards(): pl.pallas_call(functools.partial(body, (strips, cols, expos, half)), out_...  46.5 us
    unnamed x8, local copies, waits for them, and re-layouts  3.48 us

profile of v1, /device:TPU:0, one launch (start us, length us, event | category | flops | bytes accessed | tf_op | source)
XLA Modules:
  0.0 53.8 jit_solution(479409675470688480)
XLA Ops:
  0.6 0.0 copy-start
  0.6 0.1 pad.7.clone
  0.7 0.1 pad.3.clone
  0.8 0.5 copy-done
  1.3 0.1 slice.9
  1.4 0.1 rev.6
  1.6 0.0 copy-start.2
  1.6 0.7 %copy-done.2 = bf16[24,2,65]{2,1,0:T(2,128)(2,1)S(1)} copy-done((bf16[24,2,65]{2,1,0:T(2,128)(2,1)S(1)}, bf16[24,2,65]{2,1,0:T(2,128)(2,1)}, u32[]{:S(2)}) %copy-start.2) | copy-done | bytes 6264
  2.3 0.1 rev.7
  2.4 0.8 %fusion.vec_ref = f32[24,8,256]{2,1,0:T(8,128)} fusion(f32[24,2,65]{2,1,0:T(2,128)S(1)} %rev.7, f32[24,2,65]{2,1,0:T(2,128)S(1)} %convert_element_type.7, f32[24,2,64]{2,1,0:T(2,128)S(1)} %rev.6, f32[24,2,1]{2,1,0:T(2,128)S(1)} %slice.8, f32[8]{0:T(128)S(1)} %pad.7.clone, f32[8,256]{1,0:T(8,128)S(1)} %pad.3.clone), kind=kLoop, calls=%fused_computation.5 | loop fusion | flops 638976 | bytes 242272 | tf_op jit(solution)/shard_map/concatenate | solution.py:305
  3.2 46.5 %shard_map.76 = (f32[1,256,128]{2,1,0:T(8,128)}, f32[256,128]{1,0:T(8,128)}, f32[1]{0:T(128)}) custom-call(f32[1,256,128]{2,1,0:T(8,128)} %params_ref.1, s32[256,128]{1,0:T(8,128)} %target_ref.1, f32[24,8,256]{2,1,0:T(8,128)} %fusion.vec_ref, f32[24]{0:T(128)} %weight_ref.1), custom_call_target="tpu_custom_call" | custom-call | tf_op jit(solution)/shard_map/pallas_call | solution.py:320
  49.8 0.0 copy-start.1
  49.8 1.6 %copy.11 = f32[1,256,128]{2,1,0:T(8,128)} copy(f32[1,256,128]{2,1,0:T(8,128)} %get-tuple-element.6) | data formatting | bytes 262144
  51.4 0.0 copy-done.1
  51.4 0.7 %copy.12 = f32[256,128]{1,0:T(8,128)} copy(f32[256,128]{1,0:T(8,128)S(1)} %copy-done.1) | data formatting | bytes 262144
  (4 shorter events, 0.0 us)
Async XLA Ops:
  0.6 0.7 %copy-start = (bf16[24,2,65]{2,1,0:T(2,128)(2,1)S(1)}, bf16[24,2,65]{2,1,0:T(2,128)(2,1)}, u32[]{:S(2)}) copy-start(bf16[24,2,65]{2,1,0:T(2,128)(2,1)} %param.7) | copy-start | bytes 18724
  1.6 0.7 %copy-start.2 = (bf16[24,2,65]{2,1,0:T(2,128)(2,1)S(1)}, bf16[24,2,65]{2,1,0:T(2,128)(2,1)}, u32[]{:S(2)}) copy-start(bf16[24,2,65]{2,1,0:T(2,128)(2,1)} %param.8) | copy-start | bytes 18724
  49.8 1.6 %copy-start.1 = (f32[256,128]{1,0:T(8,128)S(1)}, f32[256,128]{1,0:T(8,128)}, u32[]{:S(2)}) copy-start(f32[256,128]{1,0:T(8,128)} %get-tuple-element.7) | copy-start | bytes 393220

commit v2 on v1

--- a/solution.py
+++ b/solution.py
@@ -44,7 +44,8 @@
     sizes,
     params_ref,
     target_ref,
-    vec_ref,
+    col_ref,
+    row_ref,
     weight_ref,
     new_ref,
     resist_ref,
@@ -54,7 +55,10 @@
     col_mats,
     fwd_mats,
     adj_mats,
-    columns,
+    padded,
+    lines,
+    even,
+    odd,
     fields,
     intensity,
     other,
@@ -70,7 +74,7 @@
     sum_recv,
 ):
     strips, cols, expos, half = sizes
-    kernels = vec_ref.shape[0]
+    kernels, parts, taps = col_ref.shape
     rows, width = target_ref.shape
     two = 2 * half
     wide = width + 2 * two
@@ -122,6 +126,54 @@
         to_strip, to_col = (strip + down, col + right)
         return (to_strip >= 0) & (to_strip < strips) & (to_col >= 0) & (to_col < cols)
 
+    padded[...] = jnp.zeros_like(padded)
+    for k in range(kernels):
+        for table, source in enumerate((col_ref, row_ref)):
+            padded[table, parts * k : parts * (k + 1), :taps] = source[k].astype(F32)
+    tap_ids = lax.broadcasted_iota(jnp.int32, (padded.shape[2], wide), 0)
+    places = lax.broadcasted_iota(jnp.int32, (padded.shape[2], wide), 1)
+
+    def chosen(flags):
+        return jnp.where(flags, 1.0, 0.0).astype(BF16)
+
+    col_lines, row_lines = (padded[0].astype(BF16), padded[1].astype(BF16))
+    lines[0] = dot(col_lines, chosen((tap_ids + places == wide) | (tap_ids + places == 0)))
+    lines[1] = dot(row_lines, chosen(tap_ids == places))
+    lines[2] = dot(row_lines, chosen(tap_ids + places == taps - 1))
+
+    reach = wide // 2
+
+    def circulant(table, k, part):
+        line = lines[table, pl.ds(parts * k + part, 1), :]
+        upper = pltpu.roll(
+            jnp.broadcast_to(line, (reach, wide)), 0, 1, stride=1, stride_axis=0
+        ).astype(BF16)
+        lower = jnp.concatenate([upper[:, reach:], upper[:, :reach]], axis=1)
+        return jnp.concatenate([upper, lower], axis=0)
+
+    span = adj_mats.shape[2]
+    groups = fwd_mats.shape[1]
+
+    def build_cols(k, carry):
+        for part in range(parts):
+            col_mats[k, part] = circulant(0, k, part)
+        return carry
+
+    def build_rows(k, carry):
+        t0, t1 = (circulant(1, k, part)[:span].reshape(groups, 16, wide) for part in range(2))
+        fwd_mats[k, :, 0, :, :WINDOW] = t0
+        fwd_mats[k, :, 0, :, WINDOW:] = -t1
+        fwd_mats[k, :, 1, :, :WINDOW] = t1
+        fwd_mats[k, :, 1, :, WINDOW:] = t0
+        g0, g1 = (circulant(2, k, part)[:span] for part in range(2))
+        adj_mats[k, 0, :, :WINDOW] = g0
+        adj_mats[k, 0, :, WINDOW:] = g1
+        adj_mats[k, 1, :, :WINDOW] = -g1
+        adj_mats[k, 1, :, WINDOW:] = g0
+        return carry
+
+    lax.fori_loop(0, kernels, build_cols, 0)
+
     pl.semaphore_wait(barrier, group - 1)
 
     for number, (down, right) in enumerate(DIRECTIONS):
@@ -130,30 +182,7 @@
         def _():
             transfer(number).start()
 
-    def spread(k, row, count):
-        line = vec_ref[k, row : row + 1, :]
-        return pltpu.roll(
-            jnp.broadcast_to(line, (count, line.shape[1])), 0, 1, stride=1, stride_axis=0
-        )
-
-    span = fwd_mats.shape[2]
-
-    def build(k, carry):
-        for part in range(2):
-            col_mats[k, part] = spread(k, part, wide).astype(BF16)
-        t0, t1 = (spread(k, 2, span), spread(k, 3, span))
-        fwd_mats[k, 0, :, :WINDOW] = t0.astype(BF16)
-        fwd_mats[k, 0, :, WINDOW:] = (-t1).astype(BF16)
-        fwd_mats[k, 1, :, :WINDOW] = t1.astype(BF16)
-        fwd_mats[k, 1, :, WINDOW:] = t0.astype(BF16)
-        g0, g1 = (spread(k, 4, span), spread(k, 5, span))
-        adj_mats[k, 0, :, :WINDOW] = g0.astype(BF16)
-        adj_mats[k, 0, :, WINDOW:] = g1.astype(BF16)
-        adj_mats[k, 1, :, :WINDOW] = (-g1).astype(BF16)
-        adj_mats[k, 1, :, WINDOW:] = g0.astype(BF16)
-        return carry
-
-    lax.fori_loop(0, kernels, build, 0)
+    lax.fori_loop(0, kernels, build_rows, 0)
     intensity[...] = jnp.zeros_like(intensity)
     descent[...] = jnp.zeros_like(descent)
 
@@ -171,25 +200,42 @@
     shifted = pltpu.roll(halo[0].astype(F32), lanes - (width - two), 1)
     ext[...] = shifted[:, :wide].astype(BF16)
 
-    def forward(k, carry):
-        for part in range(2):
-            columns[part] = dot(ext[...], col_mats[k, part]).astype(BF16)
+    def fill(k, held):
+        for part in range(parts):
+            held[part] = dot(ext[...], col_mats[k, part]).astype(BF16)
+
+    def use(k, held):
         weight = weight_ref[k]
         for start, count, window, offset in blocks_of(rows + two, two):
             source = jnp.concatenate(
-                [columns[0, window : window + WINDOW, :], columns[1, window : window + WINDOW, :]],
-                axis=0,
+                [held[part, window : window + WINDOW, :] for part in range(parts)], axis=0
             )
-            real_part = dot(fwd_mats[k, 0, offset : offset + count, :], source)
-            imag_part = dot(fwd_mats[k, 1, offset : offset + count, :], source)
-            fields[k, 0, start : start + count, :] = real_part
-            fields[k, 1, start : start + count, :] = imag_part
+            picked = fwd_mats[k, offset // 16 : (offset + count) // 16]
+            pair = dot(picked.reshape(2 * count, 2 * WINDOW), source)
+            pair = pair.reshape(count // 16, 2, 16, wide)
+            real_part = pair[:, 0].reshape(count, wide)
+            imag_part = pair[:, 1].reshape(count, wide)
+            fields[k, 0, start : start + count, :] = real_part.astype(BF16)
+            fields[k, 1, start : start + count, :] = imag_part.astype(BF16)
             intensity[start : start + count, :] += weight * (
                 real_part * real_part + imag_part * imag_part
             )
-        return carry
-
-    lax.fori_loop(0, kernels, forward, 0)
+
+    def in_pairs(make, take):
+        make(0, even)
+
+        def step(j, carry):
+            make(2 * j + 1, odd)
+            take(2 * j, even)
+            make(jnp.minimum(2 * j + 2, kernels - 1), even)
+            take(2 * j + 1, odd)
+            return carry
+
+        lax.fori_loop(0, kernels // 2, step, 0)
+        if kernels % 2:
+            take(kernels - 1, even)
+
+    in_pairs(fill, use)
 
     swap = pltpu.make_async_remote_copy(
         src_ref=intensity,
@@ -224,27 +270,28 @@
     own_miss = own - target_ref[...].astype(F32)
     loss_line = jnp.sum(own_miss * own_miss, axis=0, keepdims=True)
 
-    def backward(k, carry):
-        weighting = (2.0 * weight_ref[k]) * slope[...]
-        products = [(weighting * fields[k, part]).astype(BF16) for part in range(2)]
-        taps = jnp.concatenate(
-            [col_mats[k, part, two : two + width, :] for part in range(2)], axis=1
-        )
+    def correlate(k, held):
+        weighting = ((2.0 * weight_ref[k]) * slope[...]).astype(BF16)
+        products = [weighting * fields[k, part] for part in range(parts)]
         for start, count, window, offset in blocks_of(rows, two):
             source = jnp.concatenate(
-                [products[part][window : window + WINDOW, :] for part in range(2)], axis=0
+                [products[part][window : window + WINDOW, :] for part in range(parts)], axis=0
             )
-            returned = jnp.concatenate(
-                [
-                    dot(adj_mats[k, part, offset : offset + count, :], source).astype(BF16)
-                    for part in range(2)
-                ],
-                axis=1,
+            picked = jnp.concatenate(
+                [adj_mats[k, part, offset : offset + count, :] for part in range(parts)], axis=0
             )
-            descent[start : start + count, :] += dot_t(returned, taps)
-        return carry
-
-    lax.fori_loop(0, kernels, backward, 0)
+            returned = dot(picked, source).astype(BF16)
+            for part in range(parts):
+                held[part, start : start + count, :] = returned[part * count : (part + 1) * count]
+
+    def gather(k, held):
+        taps_now = jnp.concatenate(
+            [col_mats[k, part, two : two + width, :] for part in range(parts)], axis=1
+        )
+        returned = jnp.concatenate([held[part, :rows, :] for part in range(parts)], axis=1)
+        descent[...] += dot_t(returned, taps_now)
+
+    in_pairs(correlate, gather)
 
     mask = jax.nn.sigmoid(mask_slope * params_ref[0])
     gradient = descent[...] * mask_slope * mask * (1.0 - mask)
@@ -293,16 +340,6 @@
     square_sum = jnp.sum(total[1:2, :], axis=1, keepdims=True)
     root_mean = jnp.sqrt(square_sum / (expos * pixels) + norm_eps)
     new_ref[0] = params_ref[0] - step_length * descent[...] / root_mean
-
-
-def tap_lines(col_taps, row_taps, length):
-    kernels, parts, taps = col_taps.shape
-    col, row = (col_taps.astype(F32), row_taps.astype(F32))
-    gap = jnp.zeros((kernels, parts, length - taps), F32)
-    wrap = jnp.concatenate([col[..., :1], gap, col[..., :0:-1]], axis=-1)
-    ahead = jnp.concatenate([row, gap], axis=-1)
-    turned = jnp.concatenate([row[..., ::-1], gap], axis=-1)
-    return jnp.concatenate([wrap, ahead, turned, jnp.zeros_like(wrap)], axis=1)
 
 
 def shards(mask_params, target, col_taps, row_taps, kernel_weights):
@@ -324,16 +361,19 @@
             jax.ShapeDtypeStruct(target.shape, F32),
             jax.ShapeDtypeStruct((1,), F32),
         ),
-        in_specs=[vmem, vmem, vmem, smem],
+        in_specs=[vmem, vmem, vmem, vmem, smem],
         out_specs=(vmem, vmem, smem),
         scratch_shapes=[
             pltpu.VMEM((2, rows + 2 * two, 3 * width), BF16),
             pltpu.VMEM((rows + 2 * two, wide), BF16),
             pltpu.VMEM((kernels, 2, wide, wide), BF16),
+            pltpu.VMEM((kernels, span // 16, 2, 16, 2 * WINDOW), BF16),
             pltpu.VMEM((kernels, 2, span, 2 * WINDOW), BF16),
-            pltpu.VMEM((kernels, 2, span, 2 * WINDOW), BF16),
+            pltpu.VMEM((2, 2 * kernels, wide // 2), F32),
+            pltpu.VMEM((3, 2 * kernels, wide), F32),
             pltpu.VMEM((2, rows + 2 * two, wide), BF16),
-            pltpu.VMEM((kernels, 2, tall, wide), F32),
+            pltpu.VMEM((2, rows + 2 * two, wide), BF16),
+            pltpu.VMEM((kernels, 2, tall, wide), BF16),
             pltpu.VMEM((tall, wide), F32),
             pltpu.VMEM((tall, wide), F32),
             pltpu.VMEM((tall, wide), F32),
@@ -350,7 +390,7 @@
         compiler_params=pltpu.CompilerParams(
             collective_id=0, has_side_effects=True, vmem_limit_bytes=56 * 1024 * 1024
         ),
-    )(mask_params, target, tap_lines(col_taps, row_taps, wide), kernel_weights)
+    )(mask_params, target, col_taps, row_taps, kernel_weights)
 
 
 def solution(mesh):

time: 54.2 us -> 41.2 us (0.76)
  Pallas kernels: 46.5 us -> 36.5 us
  local copies, waits for them, and re-layouts: 3.97 us -> 2.26 us
  other arithmetic: 0.8 us -> 0 us
    pallas_call x1, Pallas kernels: 46.5 us -> 36.5 us  [shards(): pl.pallas_call(functools.partial(body, (strips, cols, expos, half)), out_...]
    unnamed x8 -> x4, local copies, waits for them, and re-layouts: 3.48 us -> 2.26 us
    concatenate x1 -> x0, other arithmetic: 0.79 us -> none  [tap_lines(): return jnp.concatenate([wrap, ahead, turned, jnp.zeros_like(wrap)], axis=1)]
where the time goes in v2:
time: 41.2 us; the launch traced here: 41 us
  Pallas kernels  36.5 us (89%)
  between operations  2.32 us (6%)
  local copies, waits for them, and re-layouts  2.26 us (5%)
    pallas_call x1, Pallas kernels, shards(): pl.pallas_call(functools.partial(body, (strips, cols, expos, half)), out_...  36.5 us
    unnamed x4, local copies, waits for them, and re-layouts  2.26 us

profile of v2, /device:TPU:0, one launch (start us, length us, event | category | flops | bytes accessed | tf_op | source)
XLA Modules:
  0.0 41.0 jit_solution(9700397411247015498)
XLA Ops:
  0.6 36.5 %shard_map.76 = (f32[1,256,128]{2,1,0:T(8,128)}, f32[256,128]{1,0:T(8,128)}, f32[1]{0:T(128)}) custom-call(f32[1,256,128]{2,1,0:T(8,128)} %params_ref.1, s32[256,128]{1,0:T(8,128)} %target_ref.1, bf16[24,2,65]{2,1,0:T(2,128)(2,1)} %col_ref.1, bf16[24,2,65]{2,1,0:T(2,128)(2,1)} %row_ref.1, f32[24]{0:T(128)} %weight_ref.1), custom_call_target="tpu_custom_call" | custom-call | tf_op jit(solution)/shard_map/pallas_call | solution.py:357
  37.1 0.0 copy-start
  37.1 1.6 %copy.11 = f32[1,256,128]{2,1,0:T(8,128)} copy(f32[1,256,128]{2,1,0:T(8,128)} %get-tuple-element.6) | data formatting | bytes 262144
  38.7 0.0 copy-done
  38.7 0.7 %copy.12 = f32[256,128]{1,0:T(8,128)} copy(f32[256,128]{1,0:T(8,128)S(1)} %copy-done) | data formatting | bytes 262144
Async XLA Ops:
  37.1 1.6 %copy-start = (f32[256,128]{1,0:T(8,128)S(1)}, f32[256,128]{1,0:T(8,128)}, u32[]{:S(2)}) copy-start(f32[256,128]{1,0:T(8,128)} %get-tuple-element.7) | copy-start | bytes 393220

commit v3 on v2

v3 whole, which is shorter than its diff:
```python
import functools

import jax
import jax.numpy as jnp
from jax import lax
from jax.experimental import pallas as pl
from jax.experimental.pallas import tpu as pltpu
from jax.sharding import PartitionSpec as P

mask_slope = 4.0
resist_steep = 4.0
resist_level = 3.0
step_length = 0.5
norm_eps = 1e-06

MESH = pl.DeviceIdType.MESH
F32 = jnp.float32
BF16 = jnp.bfloat16
DIRECTIONS = [(a, b) for a in (-1, 0, 1) for b in (-1, 0, 1) if (a, b) != (0, 0)]


def dot(a, b):
    return jnp.dot(a, b, preferred_element_type=F32)


def body(
    sizes,
    params_ref,
    target_ref,
    col_ref,
    row_ref,
    weight_ref,
    new_ref,
    resist_ref,
    loss_ref,
    halo,
    windows,
    padded,
    lines,
    col_mats,
    row_mats,
    row_adjoints,
    col_adjoints,
    columns,
    fields,
    intensity,
    other,
    slope,
    even,
    odd,
    descent,
    steps_ref,
    partial,
    slots,
    halo_send,
    halo_recv,
    expo_send,
    expo_recv,
    sum_send,
    sum_recv,
):
    strips, cols, expos, half = sizes
    kernels, parts, taps = col_ref.shape
    rows, width = target_ref.shape
    two = 2 * half
    tile = 2 * two
    wide = width + two
    bands = rows // tile
    group = strips * cols * expos
    strip, col, expo = (lax.axis_index("strip"), lax.axis_index("col"), lax.axis_index("expo"))
    me = (strip * cols + col) * expos + expo

    def device(index):
        return {
            "strip": index // (cols * expos),
            "col": (index // expos) % cols,
            "expo": index % expos,
        }

    halo[...] = jnp.zeros_like(halo)

    barrier = pltpu.get_barrier_semaphore()

    def greet(step, carry):
        pl.semaphore_signal(
            barrier, inc=1, device_id=device(lax.rem(me + step, group)), device_id_type=MESH
        )
        return carry

    lax.fori_loop(1, group, greet, 0)

    mask = jax.nn.sigmoid(mask_slope * params_ref[0])
    halo[0, two : two + width, tile : tile + rows] = mask.T.astype(BF16)
    target_now = target_ref[...].astype(F32)
    halo[1, two : two + width, tile : tile + rows] = target_now.T.astype(BF16)

    def transfer(number):
        down, right = DIRECTIONS[number]
        lane, lanes, to_lane = {
            -1: (tile, tile, tile + rows),
            0: (tile, rows, tile),
            1: (rows, tile, 0),
        }[down]
        place, places, to_place = {
            -1: (two, two, two + width),
            0: (two, width, two),
            1: (width, two, 0),
        }[right]
        return pltpu.make_async_remote_copy(
            src_ref=halo.at[:, pl.ds(place, places), pl.ds(lane, lanes)],
            dst_ref=halo.at[:, pl.ds(to_place, places), pl.ds(to_lane, lanes)],
            send_sem=halo_send.at[number],
            recv_sem=halo_recv.at[number],
            device_id={
                "strip": jnp.clip(strip + down, 0, strips - 1),
                "col": jnp.clip(col + right, 0, cols - 1),
            },
            device_id_type=MESH,
        )

    def inside(down, right):
        to_strip, to_col = (strip + down, col + right)
        return (to_strip >= 0) & (to_strip < strips) & (to_col >= 0) & (to_col < cols)

    padded[...] = jnp.zeros_like(padded)
    for k in range(kernels):
        for table, source in enumerate((col_ref, row_ref)):
            padded[table, parts * k : parts * (k + 1), :taps] = source[k].astype(F32)
    tap_ids = lax.broadcasted_iota(jnp.int32, (tile, tile), 0)
    places = lax.broadcasted_iota(jnp.int32, (tile, tile), 1)

    def chosen(flags):
        return jnp.where(flags, 1.0, 0.0).astype(BF16)

    col_lines, row_lines = (padded[0].astype(BF16), padded[1].astype(BF16))
    last = taps - 1
    lines[0] = dot(row_lines, chosen((tap_ids + places == tile) | (tap_ids + places == 0)))
    lines[1] = dot(
        row_lines, chosen((places - tap_ids == tile - last) | (tap_ids - places == last))
    )
    lines[2] = dot(col_lines, chosen(tap_ids + places == last))
    lower = tap_ids >= places
    upper = tap_ids <= places

    def rolled(line, count):
        return pltpu.roll(
            jnp.broadcast_to(line, (count, tile)), 0, 1, stride=1, stride_axis=0
        )

    def circulant(table, k, part):
        return rolled(lines[table, pl.ds(parts * k + part, 1), :], tile)

    def build_cols(k, carry):
        for part in range(parts):
            line = padded[0, pl.ds(parts * k + part, 1), :]
            col_mats[k, part * two : (part + 1) * two, :] = rolled(line, two).astype(BF16)
        return carry

    def build_rows(k, carry):
        t0, t1 = (circulant(0, k, part) for part in range(parts))
        for half_id, keep in enumerate((lower, ~lower)):
            a0, a1 = (jnp.where(keep, t, 0.0).astype(BF16) for t in (t0, t1))
            top = 2 * tile * half_id
            row_mats[k, top : top + tile, :tile] = a0
            row_mats[k, top : top + tile, tile:] = a1
            row_mats[k, top + tile : top + 2 * tile, :tile] = -a1
            row_mats[k, top + tile : top + 2 * tile, tile:] = a0
        return carry

    def build_adjoints(k, carry):
        t0, t1 = (circulant(1, k, part) for part in range(parts))
        for half_id, keep in enumerate((lower, ~lower)):
            a0, a1 = (jnp.where(keep, t, 0.0).astype(BF16) for t in (t0, t1))
            top = 2 * tile * half_id
            row_adjoints[k, top : top + tile, :tile] = a0
            row_adjoints[k, top : top + tile, tile:] = -a1
            row_adjoints[k, top + tile : top + 2 * tile, :tile] = a1
            row_adjoints[k, top + tile : top + 2 * tile, tile:] = a0
        u0, u1 = (circulant(2, k, part) for part in range(parts))
        col_adjoints[k, :, :tile] = jnp.where(upper, u0, 0.0).astype(BF16)
        col_adjoints[k, :, tile : 2 * tile] = jnp.where(upper, u1, 0.0).astype(BF16)
        r0 = jnp.where(upper, 0.0, u0)
        r1 = pltpu.roll(jnp.where(upper, 0.0, u1), two, 1)
        col_adjoints[k, :, 2 * tile :] = jnp.where(places < two, r0, r1).astype(BF16)
        return carry

    lax.fori_loop(0, kernels, build_cols, 0)

    pl.semaphore_wait(barrier, group - 1)

    for number, (down, right) in enumerate(DIRECTIONS):

        @pl.when(inside(down, right))
        def _():
            transfer(number).start()

    lax.fori_loop(0, kernels, build_rows, 0)
    intensity[...] = jnp.zeros_like(intensity)
    descent[...] = jnp.zeros_like(descent)

    for number, (down, right) in enumerate(DIRECTIONS):

        @pl.when(inside(down, right))
        def _():
            transfer(number).wait_send()

        @pl.when(inside(-down, -right))
        def _():
            transfer(number).wait_recv()

    lanes = halo.shape[2]
    reach = rows + tile
    shifted = pltpu.roll(halo[0].astype(F32), lanes - two, 1)[:, :reach].astype(BF16)
    steps = wide // two
    for step in range(steps):
        windows[:, step * reach : (step + 1) * reach] = shifted[step * two : step * two + tile]

    batch = next(size for size in (4, 3, 2, 1) if kernels % size == 0)

    def col_pass(j, carry):
        first = j * batch
        made = dot(
            col_mats[pl.ds(first, batch)].reshape(batch * parts * two, tile), windows[...]
        ).astype(BF16)
        for i in range(batch):
            for part in range(parts):
                top = (i * parts + part) * two
                for step in range(steps):
                    for band in range(bands + 1):
                        lane = step * reach + band * tile
                        columns[
                            first + i,
                            band,
                            step * two : (step + 1) * two,
                            part * tile : (part + 1) * tile,
                        ] = made[top : top + two, lane : lane + tile]
        return carry

    lax.fori_loop(0, kernels // batch, col_pass, 0)

    def row_pass(k):
        weight = weight_ref[k]
        held = [columns[k, band] for band in range(bands + 1)]
        joined = jnp.concatenate(
            [jnp.concatenate(held[band : band + 2], axis=1) for band in range(bands)], axis=0
        )
        whole = dot(joined, row_mats[k])
        tail = dot(held[bands], row_mats[k, : 2 * tile, :])
        for band in range(bands + 1):
            pair = tail if band == bands else whole[band * wide : (band + 1) * wide]
            fields[k, band] = pair.astype(BF16)
            real_part, imag_part = (pair[:, :tile], pair[:, tile:])
            intensity[band] += weight * (real_part * real_part + imag_part * imag_part)

    unroll = next(size for size in (2, 1) if kernels % size == 0)

    def row_passes(j, carry):
        for i in range(unroll):
            row_pass(j * unroll + i)
        return carry

    lax.fori_loop(0, kernels // unroll, row_passes, 0)

    def in_pairs(make, take):
        make(0, even)

        def step(j, carry):
            make(2 * j + 1, odd)
            take(2 * j, even)
            make(jnp.minimum(2 * j + 2, kernels - 1), even)
            take(2 * j + 1, odd)
            return carry

        lax.fori_loop(0, kernels // 2, step, 0)
        if kernels % 2:
            take(kernels - 1, even)

    swap = pltpu.make_async_remote_copy(
        src_ref=intensity,
        dst_ref=other,
        send_sem=expo_send,
        recv_sem=expo_recv,
        device_id={"expo": 1 - expo},
        device_id_type=MESH,
    )
    swap.start()
    lax.fori_loop(0, kernels, build_adjoints, 0)
    swap.wait()

    def side_by_side(ref):
        return jnp.concatenate([ref[band] for band in range(bands + 1)], axis=1)

    total = side_by_side(intensity) + side_by_side(other)
    resist = jax.nn.sigmoid(resist_steep * (total - resist_level))
    target_ext = pltpu.roll(
        halo[1, half : half + wide, :].astype(F32), lanes - (tile - half), 1
    )[:, :reach]
    row_lanes = lax.broadcasted_iota(jnp.int32, (wide, reach), 1)
    row_ids = row_lanes + (strip * rows - half)
    col_ids = lax.broadcasted_iota(jnp.int32, (wide, reach), 0) + (col * width - half)
    kept = (
        (row_ids >= 0)
        & (row_ids < strips * rows)
        & (col_ids >= 0)
        & (col_ids < cols * width)
        & (row_lanes < rows + two)
    )
    mismatch = resist - target_ext
    steepness = jnp.where(kept, 2.0 * mismatch * resist_steep * resist * (1.0 - resist), 0.0)
    for band in range(bands + 1):
        slope[band] = steepness[:, band * tile : (band + 1) * tile]
    own = pltpu.roll(resist[half : half + width, :], reach - half, 1)[:, :rows].T
    resist_ref[...] = own
    own_miss = own - target_ref[...].astype(F32)
    loss_line = jnp.sum(own_miss * own_miss, axis=0, keepdims=True)

    def correlate(k, held):
        scale = 2.0 * weight_ref[k]
        products = []
        for band in range(bands + 1):
            weighting = (scale * slope[band]).astype(BF16)
            products.append(fields[k, band] * jnp.concatenate([weighting] * parts, axis=1))
        joined = jnp.concatenate(
            [jnp.concatenate(products[band : band + 2], axis=1) for band in range(bands)], axis=0
        )
        returned = dot(joined, row_adjoints[k]).astype(BF16)
        for band in range(bands):
            held[band] = returned[band * wide : (band + 1) * wide]

    def gather(k, held):
        found = [
            jnp.concatenate(
                [held[band, :, part * tile : (part + 1) * tile] for band in range(bands)], axis=1
            )
            for part in range(parts)
        ]
        source = jnp.concatenate([f[:tile] for f in found] + [f[tile:] for f in found], axis=0)
        descent[...] += dot(col_adjoints[k], source)

    in_pairs(correlate, gather)

    mask = jax.nn.sigmoid(mask_slope * params_ref[0])
    gradient = descent[...].T * mask_slope * mask * (1.0 - mask)
    steps_ref[...] = gradient
    square_line = jnp.sum(gradient * gradient, axis=0, keepdims=True)
    which = lax.broadcasted_iota(jnp.int32, partial.shape, 0)
    sums = jnp.where(which == 0, loss_line, jnp.where(which == 1, square_line, 0.0))
    partial[...] = sums
    slots[me] = sums

    def share(step):
        return pltpu.make_async_remote_copy(
            src_ref=partial,
            dst_ref=slots.at[me],
            send_sem=sum_send.at[step],
            recv_sem=sum_recv.at[me],
            device_id=device(lax.rem(me + step, group)),
            device_id_type=MESH,
        )

    def arrival(step):
        source = lax.rem(me + step, group)
        return pltpu.make_async_remote_copy(
            src_ref=partial,
            dst_ref=slots.at[source],
            send_sem=sum_send.at[step],
            recv_sem=sum_recv.at[source],
            device_id=device(source),
            device_id_type=MESH,
        )

    def send_sums(step, carry):
        share(step).start()
        return carry

    def wait_sums(step, carry):
        arrival(step).wait()
        return carry

    lax.fori_loop(1, group, send_sums, 0)
    lax.fori_loop(1, group, wait_sums, 0)

    totals = jnp.sum(slots[...], axis=0)
    pixels = rows * width * strips * cols
    loss_ref[0] = jnp.sum(totals[0:1, :]) / (expos * pixels)
    square_sum = jnp.sum(totals[1:2, :], axis=1, keepdims=True)
    root_mean = jnp.sqrt(square_sum / (expos * pixels) + norm_eps)
    new_ref[0] = params_ref[0] - step_length * steps_ref[...] / root_mean


def shards(mask_params, target, col_taps, row_taps, kernel_weights):
    rows, width = target.shape
    kernels, _, taps = col_taps.shape
    half = taps // 2
    two = 2 * half
    tile, wide, bands = (2 * two, width + two, rows // (2 * two))
    strips, cols, expos = (lax.axis_size(a) for a in ("strip", "col", "expo"))
    group = strips * cols * expos
    vmem = pl.BlockSpec(memory_space=pltpu.VMEM)
    smem = pl.BlockSpec(memory_space=pltpu.SMEM)
    dma = pltpu.SemaphoreType.DMA
    return pl.pallas_call(
        functools.partial(body, (strips, cols, expos, half)),
        out_shape=(
            jax.ShapeDtypeStruct(mask_params.shape, F32),
            jax.ShapeDtypeStruct(target.shape, F32),
            jax.ShapeDtypeStruct((1,), F32),
        ),
        in_specs=[vmem, vmem, vmem, vmem, smem],
        out_specs=(vmem, vmem, smem),
        scratch_shapes=[
            pltpu.VMEM((2, width + 2 * two, rows + 2 * tile), BF16),
            pltpu.VMEM((tile, (wide // two) * (rows + tile)), BF16),
            pltpu.VMEM((2, 2 * kernels, tile), F32),
            pltpu.VMEM((3, 2 * kernels, tile), F32),
            pltpu.VMEM((kernels, 2 * two, tile), BF16),
            pltpu.VMEM((kernels, 4 * tile, 2 * tile), BF16),
            pltpu.VMEM((kernels, 4 * tile, 2 * tile), BF16),
            pltpu.VMEM((kernels, width, 3 * tile), BF16),
            pltpu.VMEM((kernels, bands + 1, wide, 2 * tile), BF16),
            pltpu.VMEM((kernels, bands + 1, wide, 2 * tile), BF16),
            pltpu.VMEM((bands + 1, wide, tile), F32),
            pltpu.VMEM((bands + 1, wide, tile), F32),
            pltpu.VMEM((bands + 1, wide, tile), F32),
            pltpu.VMEM((bands, wide, 2 * tile), BF16),
            pltpu.VMEM((bands, wide, 2 * tile), BF16),
            pltpu.VMEM((width, rows), F32),
            pltpu.VMEM((rows, width), F32),
            pltpu.VMEM((8, width), F32),
            pltpu.VMEM((group, 8, width), F32),
            dma((8,)),
            dma((8,)),
            dma,
            dma,
            dma((group,)),
            dma((group,)),
        ],
        compiler_params=pltpu.CompilerParams(
            collective_id=0, has_side_effects=True, vmem_limit_bytes=56 * 1024 * 1024
        ),
    )(mask_params, target, col_taps, row_taps, kernel_weights)


def solution(mesh):
    return jax.shard_map(
        shards,
        mesh=mesh,
        in_specs=(
            P("expo", ("tiles", "strip"), "col"),
            P(("tiles", "strip"), "col"),
            P(),
            P(),
            P(),
        ),
        out_specs=(P("expo", ("tiles", "strip"), "col"), P(("tiles", "strip"), "col"), P("tiles")),
        check_vma=False,
    )
```

time: 41.2 us -> 41.3 us (level)
  no operation moved by 1% of the time
where the time goes in v3:
time: 41.3 us; the launch traced here: 41.1 us
  Pallas kernels  36.5 us (88%)
  between operations  2.32 us (6%)
  local copies, waits for them, and re-layouts  2.26 us (5%)
    pallas_call x1, Pallas kernels, shards(): pl.pallas_call(functools.partial(body, (strips, cols, expos, half)), out_...  36.5 us
    unnamed x4, local copies, waits for them, and re-layouts  2.26 us

profile of v3, /device:TPU:0, one launch (start us, length us, event | category | flops | bytes accessed | tf_op | source)
XLA Modules:
  0.0 41.1 jit_solution(9267488073446946355)
XLA Ops:
  0.6 36.5 %shard_map.76 = (f32[1,256,128]{2,1,0:T(8,128)}, f32[256,128]{1,0:T(8,128)}, f32[1]{0:T(128)}) custom-call(f32[1,256,128]{2,1,0:T(8,128)} %params_ref.1, s32[256,128]{1,0:T(8,128)} %target_ref.1, bf16[24,2,65]{2,1,0:T(2,128)(2,1)} %col_ref.1, bf16[24,2,65]{2,1,0:T(2,128)(2,1)} %row_ref.1, f32[24]{0:T(128)} %weight_ref.1), custom_call_target="tpu_custom_call" | custom-call | tf_op jit(solution)/shard_map/pallas_call | solution.py:402
  37.1 0.0 copy-start
  37.2 1.6 %copy.11 = f32[1,256,128]{2,1,0:T(8,128)} copy(f32[1,256,128]{2,1,0:T(8,128)} %get-tuple-element.6) | data formatting | bytes 262144
  38.8 0.0 copy-done
  38.8 0.7 %copy.12 = f32[256,128]{1,0:T(8,128)} copy(f32[256,128]{1,0:T(8,128)S(1)} %copy-done) | data formatting | bytes 262144
Async XLA Ops:
  37.1 1.6 %copy-start = (f32[256,128]{1,0:T(8,128)S(1)}, f32[256,128]{1,0:T(8,128)}, u32[]{:S(2)}) copy-start(f32[256,128]{1,0:T(8,128)} %get-tuple-element.7) | copy-start | bytes 393220

commit v4 on v3

--- a/solution.py
+++ b/solution.py
@@ -37,6 +37,7 @@
     windows,
     padded,
     lines,
+    masks,
     col_mats,
     row_mats,
     row_adjoints,
@@ -139,8 +140,10 @@
         row_lines, chosen((places - tap_ids == tile - last) | (tap_ids - places == last))
     )
     lines[2] = dot(col_lines, chosen(tap_ids + places == last))
-    lower = tap_ids >= places
-    upper = tap_ids <= places
+    masks[0] = chosen(tap_ids >= places)
+    masks[1] = chosen(tap_ids < places)
+    masks[2] = chosen(tap_ids <= places)
+    masks[3] = chosen(tap_ids > jnp.where(places < two, places, places - two))
 
     def rolled(line, count):
         return pltpu.roll(
@@ -156,33 +159,35 @@
             col_mats[k, part * two : (part + 1) * two, :] = rolled(line, two).astype(BF16)
         return carry
 
+    def triangles(table, k, kept):
+        t0, t1 = (circulant(table, k, part).astype(BF16) for part in range(parts))
+        for side in range(2):
+            a1 = t1 * masks[side]
+            kept[k, side, 0] = t0 * masks[side]
+            kept[k, side, 1] = a1
+            kept[k, side, 2] = -a1
+
     def build_rows(k, carry):
-        t0, t1 = (circulant(0, k, part) for part in range(parts))
-        for half_id, keep in enumerate((lower, ~lower)):
-            a0, a1 = (jnp.where(keep, t, 0.0).astype(BF16) for t in (t0, t1))
-            top = 2 * tile * half_id
-            row_mats[k, top : top + tile, :tile] = a0
-            row_mats[k, top : top + tile, tile:] = a1
-            row_mats[k, top + tile : top + 2 * tile, :tile] = -a1
-            row_mats[k, top + tile : top + 2 * tile, tile:] = a0
-        return carry
-
-    def build_adjoints(k, carry):
-        t0, t1 = (circulant(1, k, part) for part in range(parts))
-        for half_id, keep in enumerate((lower, ~lower)):
-            a0, a1 = (jnp.where(keep, t, 0.0).astype(BF16) for t in (t0, t1))
-            top = 2 * tile * half_id
-            row_adjoints[k, top : top + tile, :tile] = a0
-            row_adjoints[k, top : top + tile, tile:] = -a1
-            row_adjoints[k, top + tile : top + 2 * tile, :tile] = a1
-            row_adjoints[k, top + tile : top + 2 * tile, tile:] = a0
+        triangles(0, k, row_mats)
+        return carry
+
+    def build_adjoints(k):
+        triangles(1, k, row_adjoints)
         u0, u1 = (circulant(2, k, part) for part in range(parts))
-        col_adjoints[k, :, :tile] = jnp.where(upper, u0, 0.0).astype(BF16)
-        col_adjoints[k, :, tile : 2 * tile] = jnp.where(upper, u1, 0.0).astype(BF16)
-        r0 = jnp.where(upper, 0.0, u0)
-        r1 = pltpu.roll(jnp.where(upper, 0.0, u1), two, 1)
-        col_adjoints[k, :, 2 * tile :] = jnp.where(places < two, r0, r1).astype(BF16)
-        return carry
+        col_adjoints[k, :, :tile] = u0.astype(BF16) * masks[2]
+        col_adjoints[k, :, tile : 2 * tile] = u1.astype(BF16) * masks[2]
+        mixed = jnp.where(places < two, u0, pltpu.roll(u1, two, 1)).astype(BF16)
+        col_adjoints[k, :, 2 * tile :] = mixed * masks[3]
+
+    def square(kept, k, side, top, bottom):
+        plain = kept[k, side, 0]
+        return jnp.concatenate(
+            [
+                jnp.concatenate([plain, kept[k, side, top]], axis=1),
+                jnp.concatenate([kept[k, side, bottom], plain], axis=1),
+            ],
+            axis=0,
+        )
 
     lax.fori_loop(0, kernels, build_cols, 0)
 
@@ -244,36 +249,38 @@
         joined = jnp.concatenate(
             [jnp.concatenate(held[band : band + 2], axis=1) for band in range(bands)], axis=0
         )
-        whole = dot(joined, row_mats[k])
-        tail = dot(held[bands], row_mats[k, : 2 * tile, :])
+        first, second = (square(row_mats, k, side, 1, 2) for side in range(2))
+        whole = dot(joined, jnp.concatenate([first, second], axis=0))
+        tail = dot(held[bands], first)
         for band in range(bands + 1):
             pair = tail if band == bands else whole[band * wide : (band + 1) * wide]
             fields[k, band] = pair.astype(BF16)
             real_part, imag_part = (pair[:, :tile], pair[:, tile:])
             intensity[band] += weight * (real_part * real_part + imag_part * imag_part)
 
-    unroll = next(size for size in (2, 1) if kernels % size == 0)
+    unroll = next(size for size in (4, 3, 2, 1) if kernels % size == 0)
 
     def row_passes(j, carry):
         for i in range(unroll):
             row_pass(j * unroll + i)
+            build_adjoints(j * unroll + i)
         return carry
 
     lax.fori_loop(0, kernels // unroll, row_passes, 0)
 
     def in_pairs(make, take):
         make(0, even)
+        helds = (even, odd)
+        size = next(size for size in (4, 2, 1) if kernels % size == 0)
 
         def step(j, carry):
-            make(2 * j + 1, odd)
-            take(2 * j, even)
-            make(jnp.minimum(2 * j + 2, kernels - 1), even)
-            take(2 * j + 1, odd)
+            for i in range(size):
+                k = size * j + i
+                make(jnp.minimum(k + 1, kernels - 1), helds[(i + 1) % 2])
+                take(k, helds[i % 2])
             return carry
 
-        lax.fori_loop(0, kernels // 2, step, 0)
-        if kernels % 2:
-            take(kernels - 1, even)
+        lax.fori_loop(0, kernels // size, step, 0)
 
     swap = pltpu.make_async_remote_copy(
         src_ref=intensity,
@@ -284,7 +291,6 @@
         device_id_type=MESH,
     )
     swap.start()
-    lax.fori_loop(0, kernels, build_adjoints, 0)
     swap.wait()
 
     def side_by_side(ref):
@@ -323,7 +329,10 @@
         joined = jnp.concatenate(
             [jnp.concatenate(products[band : band + 2], axis=1) for band in range(bands)], axis=0
         )
-        returned = dot(joined, row_adjoints[k]).astype(BF16)
+        matrix = jnp.concatenate(
+            [square(row_adjoints, k, side, 2, 1) for side in range(2)], axis=0
+        )
+        returned = dot(joined, matrix).astype(BF16)
         for band in range(bands):
             held[band] = returned[band * wide : (band + 1) * wide]
 
@@ -413,9 +422,10 @@
             pltpu.VMEM((tile, (wide // two) * (rows + tile)), BF16),
             pltpu.VMEM((2, 2 * kernels, tile), F32),
             pltpu.VMEM((3, 2 * kernels, tile), F32),
+            pltpu.VMEM((4, tile, tile), BF16),
             pltpu.VMEM((kernels, 2 * two, tile), BF16),
-            pltpu.VMEM((kernels, 4 * tile, 2 * tile), BF16),
-            pltpu.VMEM((kernels, 4 * tile, 2 * tile), BF16),
+            pltpu.VMEM((kernels, 2, 3, tile, tile), BF16),
+            pltpu.VMEM((kernels, 2, 3, tile, tile), BF16),
             pltpu.VMEM((kernels, width, 3 * tile), BF16),
             pltpu.VMEM((kernels, bands + 1, wide, 2 * tile), BF16),
             pltpu.VMEM((kernels, bands + 1, wide, 2 * tile), BF16),

time: 41.3 us -> 35.5 us (0.86)
  Pallas kernels: 36.5 us -> 30.7 us
    pallas_call x1, Pallas kernels: 36.5 us -> 30.7 us  [shards(): pl.pallas_call(functools.partial(body, (strips, cols, expos, half)), out_...]
where the time goes in v4:
time: 35.5 us; the launch traced here: 35.3 us
  Pallas kernels  30.7 us (86%)
  between operations  2.32 us (7%)
  local copies, waits for them, and re-layouts  2.26 us (6%)
    pallas_call x1, Pallas kernels, shards(): pl.pallas_call(functools.partial(body, (strips, cols, expos, half)), out_...  30.7 us
    unnamed x4, local copies, waits for them, and re-layouts  2.26 us

profile of v4, /device:TPU:0, one launch (start us, length us, event | category | flops | bytes accessed | tf_op | source)
XLA Modules:
  0.0 35.3 jit_solution(13951982705673057630)
XLA Ops:
  0.6 30.7 %shard_map.76 = (f32[1,256,128]{2,1,0:T(8,128)}, f32[256,128]{1,0:T(8,128)}, f32[1]{0:T(128)}) custom-call(f32[1,256,128]{2,1,0:T(8,128)} %params_ref.1, s32[256,128]{1,0:T(8,128)} %target_ref.1, bf16[24,2,65]{2,1,0:T(2,128)(2,1)} %col_ref.1, bf16[24,2,65]{2,1,0:T(2,128)(2,1)} %row_ref.1, f32[24]{0:T(128)} %weight_ref.1), custom_call_target="tpu_custom_call" | custom-call | tf_op jit(solution)/shard_map/pallas_call | solution.py:411
  31.4 0.0 copy-start
  31.4 1.6 %copy.11 = f32[1,256,128]{2,1,0:T(8,128)} copy(f32[1,256,128]{2,1,0:T(8,128)} %get-tuple-element.6) | data formatting | bytes 262144
  33.0 0.0 copy-done
  33.0 0.7 %copy.12 = f32[256,128]{1,0:T(8,128)} copy(f32[256,128]{1,0:T(8,128)S(1)} %copy-done) | data formatting | bytes 262144
Async XLA Ops:
  31.4 1.6 %copy-start = (f32[256,128]{1,0:T(8,128)S(1)}, f32[256,128]{1,0:T(8,128)}, u32[]{:S(2)}) copy-start(f32[256,128]{1,0:T(8,128)} %get-tuple-element.7) | copy-start | bytes 393220

commit v5 on v4

--- a/solution.py
+++ b/solution.py
@@ -25,14 +25,16 @@
 
 def body(
     sizes,
-    params_ref,
-    target_ref,
+    params_hbm,
+    target_hbm,
     col_ref,
     row_ref,
     weight_ref,
-    new_ref,
+    steps_ref,
     resist_ref,
-    loss_ref,
+    totals_ref,
+    params_ref,
+    target_ref,
     halo,
     windows,
     padded,
@@ -42,7 +44,8 @@
     row_mats,
     row_adjoints,
     col_adjoints,
-    columns,
+    even_columns,
+    odd_columns,
     fields,
     intensity,
     other,
@@ -50,9 +53,9 @@
     even,
     odd,
     descent,
-    steps_ref,
     partial,
     slots,
+    fetch_sem,
     halo_send,
     halo_recv,
     expo_send,
@@ -71,25 +74,42 @@
     strip, col, expo = (lax.axis_index("strip"), lax.axis_index("col"), lax.axis_index("expo"))
     me = (strip * cols + col) * expos + expo
 
-    def device(index):
-        return {
-            "strip": index // (cols * expos),
-            "col": (index // expos) % cols,
-            "expo": index % expos,
-        }
+    def beyond(index, step, count):
+        moved = index + step
+        return jnp.where(moved >= count, moved - count, moved)
+
+    peers = []
+    for number in range(1, group):
+        steps_to = (number // (cols * expos), number // expos % cols, number % expos)
+        there = [
+            beyond(index, step, count) if step else index
+            for index, step, count in zip((strip, col, expo), steps_to, sizes[:3])
+        ]
+        peers.append(
+            (
+                dict(zip(("strip", "col", "expo"), there)),
+                (there[0] * cols + there[1]) * expos + there[2],
+            )
+        )
+
+    fetches = [
+        pltpu.make_async_copy(source, into, fetch_sem.at[number])
+        for number, (source, into) in enumerate(
+            ((params_hbm, params_ref), (target_hbm, target_ref))
+        )
+    ]
+    for fetch in fetches:
+        fetch.start()
 
     halo[...] = jnp.zeros_like(halo)
 
     barrier = pltpu.get_barrier_semaphore()
 
-    def greet(step, carry):
-        pl.semaphore_signal(
-            barrier, inc=1, device_id=device(lax.rem(me + step, group)), device_id_type=MESH
-        )
-        return carry
-
-    lax.fori_loop(1, group, greet, 0)
-
+    for place, _ in peers:
+        pl.semaphore_signal(barrier, inc=1, device_id=place, device_id_type=MESH)
+
+    for fetch in fetches:
+        fetch.wait()
     mask = jax.nn.sigmoid(mask_slope * params_ref[0])
     halo[0, two : two + width, tile : tile + rows] = mask.T.astype(BF16)
     target_now = target_ref[...].astype(F32)
@@ -222,7 +242,7 @@
 
     batch = next(size for size in (4, 3, 2, 1) if kernels % size == 0)
 
-    def col_pass(j, carry):
+    def col_pass(j, held):
         first = j * batch
         made = dot(
             col_mats[pl.ds(first, batch)].reshape(batch * parts * two, tile), windows[...]
@@ -233,19 +253,16 @@
                 for step in range(steps):
                     for band in range(bands + 1):
                         lane = step * reach + band * tile
-                        columns[
-                            first + i,
+                        held[
+                            i,
                             band,
                             step * two : (step + 1) * two,
                             part * tile : (part + 1) * tile,
                         ] = made[top : top + two, lane : lane + tile]
-        return carry
-
-    lax.fori_loop(0, kernels // batch, col_pass, 0)
-
-    def row_pass(k):
+
+    def row_pass(k, columns):
         weight = weight_ref[k]
-        held = [columns[k, band] for band in range(bands + 1)]
+        held = [columns[band] for band in range(bands + 1)]
         joined = jnp.concatenate(
             [jnp.concatenate(held[band : band + 2], axis=1) for band in range(bands)], axis=0
         )
@@ -258,29 +275,28 @@
             real_part, imag_part = (pair[:, :tile], pair[:, tile:])
             intensity[band] += weight * (real_part * real_part + imag_part * imag_part)
 
-    unroll = next(size for size in (4, 3, 2, 1) if kernels % size == 0)
-
-    def row_passes(j, carry):
-        for i in range(unroll):
-            row_pass(j * unroll + i)
-            build_adjoints(j * unroll + i)
-        return carry
-
-    lax.fori_loop(0, kernels // unroll, row_passes, 0)
-
-    def in_pairs(make, take):
-        make(0, even)
-        helds = (even, odd)
-        size = next(size for size in (4, 2, 1) if kernels % size == 0)
+    def row_passes(j, held):
+        for i in range(batch):
+            row_pass(j * batch + i, held.at[i])
+            build_adjoints(j * batch + i)
+
+    def in_pairs(make, take, count, helds):
+        make(0, helds[0])
+        size = next(size for size in (4, 2, 1) if count % size == 0)
 
         def step(j, carry):
             for i in range(size):
                 k = size * j + i
-                make(jnp.minimum(k + 1, kernels - 1), helds[(i + 1) % 2])
-                take(k, helds[i % 2])
+                if size == 1:
+                    take(k, helds[0])
+                make(jnp.minimum(k + 1, count - 1), helds[(i + 1) % 2 if size > 1 else 0])
+                if size > 1:
+                    take(k, helds[i % 2])
             return carry
 
-        lax.fori_loop(0, kernels // size, step, 0)
+        lax.fori_loop(0, count // size, step, 0)
+
+    in_pairs(col_pass, row_passes, kernels // batch, (even_columns, odd_columns))
 
     swap = pltpu.make_async_remote_copy(
         src_ref=intensity,
@@ -346,7 +362,7 @@
         source = jnp.concatenate([f[:tile] for f in found] + [f[tile:] for f in found], axis=0)
         descent[...] += dot(col_adjoints[k], source)
 
-    in_pairs(correlate, gather)
+    in_pairs(correlate, gather, kernels, (even, odd))
 
     mask = jax.nn.sigmoid(mask_slope * params_ref[0])
     gradient = descent[...].T * mask_slope * mask * (1.0 - mask)
@@ -357,44 +373,36 @@
     partial[...] = sums
     slots[me] = sums
 
-    def share(step):
-        return pltpu.make_async_remote_copy(
-            src_ref=partial,
-            dst_ref=slots.at[me],
-            send_sem=sum_send.at[step],
-            recv_sem=sum_recv.at[me],
-            device_id=device(lax.rem(me + step, group)),
-            device_id_type=MESH,
-        )
-
-    def arrival(step):
-        source = lax.rem(me + step, group)
-        return pltpu.make_async_remote_copy(
-            src_ref=partial,
-            dst_ref=slots.at[source],
-            send_sem=sum_send.at[step],
-            recv_sem=sum_recv.at[source],
-            device_id=device(source),
-            device_id_type=MESH,
-        )
-
-    def send_sums(step, carry):
-        share(step).start()
-        return carry
-
-    def wait_sums(step, carry):
-        arrival(step).wait()
-        return carry
-
-    lax.fori_loop(1, group, send_sums, 0)
-    lax.fori_loop(1, group, wait_sums, 0)
-
-    totals = jnp.sum(slots[...], axis=0)
-    pixels = rows * width * strips * cols
-    loss_ref[0] = jnp.sum(totals[0:1, :]) / (expos * pixels)
-    square_sum = jnp.sum(totals[1:2, :], axis=1, keepdims=True)
+    shares, arrivals = ([], [])
+    for number, (place, index) in enumerate(peers):
+        for found, slot in ((shares, me), (arrivals, index)):
+            found.append(
+                pltpu.make_async_remote_copy(
+                    src_ref=partial,
+                    dst_ref=slots.at[slot],
+                    send_sem=sum_send.at[number],
+                    recv_sem=sum_recv.at[slot],
+                    device_id=place,
+                    device_id_type=MESH,
+                )
+            )
+    for share in shares:
+        share.start()
+    for arrival in arrivals:
+        arrival.wait()
+
+    totals_ref[...] = jnp.sum(slots[...], axis=0)
+
+
+def finish(copies, params_ref, steps_ref, resist_in, totals_ref, new_ref, resist_ref, loss_ref):
+    expos, blocks = copies
+    rows, width = resist_in.shape
+    pixels = rows * width * blocks
+    loss_ref[0] = jnp.sum(totals_ref[0:1, :]) / (expos * pixels)
+    square_sum = jnp.sum(totals_ref[1:2, :], axis=1, keepdims=True)
     root_mean = jnp.sqrt(square_sum / (expos * pixels) + norm_eps)
     new_ref[0] = params_ref[0] - step_length * steps_ref[...] / root_mean
+    resist_ref[...] = resist_in[...]
 
 
 def shards(mask_params, target, col_taps, row_taps, kernel_weights):
@@ -408,16 +416,17 @@
     vmem = pl.BlockSpec(memory_space=pltpu.VMEM)
     smem = pl.BlockSpec(memory_space=pltpu.SMEM)
     dma = pltpu.SemaphoreType.DMA
-    return pl.pallas_call(
+    image = jax.ShapeDtypeStruct(target.shape, F32)
+    batch = next(size for size in (4, 3, 2, 1) if kernels % size == 0)
+    anywhere = pl.BlockSpec(memory_space=pl.ANY)
+    steps, resist, totals = pl.pallas_call(
         functools.partial(body, (strips, cols, expos, half)),
-        out_shape=(
-            jax.ShapeDtypeStruct(mask_params.shape, F32),
-            jax.ShapeDtypeStruct(target.shape, F32),
-            jax.ShapeDtypeStruct((1,), F32),
-        ),
-        in_specs=[vmem, vmem, vmem, vmem, smem],
-        out_specs=(vmem, vmem, smem),
+        out_shape=(image, image, jax.ShapeDtypeStruct((8, width), F32)),
+        in_specs=[anywhere, anywhere, vmem, vmem, smem],
+        out_specs=(vmem, vmem, vmem),
         scratch_shapes=[
+            pltpu.VMEM(mask_params.shape, F32),
+            pltpu.VMEM(target.shape, target.dtype),
             pltpu.VMEM((2, width + 2 * two, rows + 2 * tile), BF16),
             pltpu.VMEM((tile, (wide // two) * (rows + tile)), BF16),
             pltpu.VMEM((2, 2 * kernels, tile), F32),
@@ -427,7 +436,8 @@
             pltpu.VMEM((kernels, 2, 3, tile, tile), BF16),
             pltpu.VMEM((kernels, 2, 3, tile, tile), BF16),
             pltpu.VMEM((kernels, width, 3 * tile), BF16),
-            pltpu.VMEM((kernels, bands + 1, wide, 2 * tile), BF16),
+            pltpu.VMEM((batch, bands + 1, wide, 2 * tile), BF16),
+            pltpu.VMEM((batch, bands + 1, wide, 2 * tile), BF16),
             pltpu.VMEM((kernels, bands + 1, wide, 2 * tile), BF16),
             pltpu.VMEM((bands + 1, wide, tile), F32),
             pltpu.VMEM((bands + 1, wide, tile), F32),
@@ -435,9 +445,9 @@
             pltpu.VMEM((bands, wide, 2 * tile), BF16),
             pltpu.VMEM((bands, wide, 2 * tile), BF16),
             pltpu.VMEM((width, rows), F32),
-            pltpu.VMEM((rows, width), F32),
             pltpu.VMEM((8, width), F32),
             pltpu.VMEM((group, 8, width), F32),
+            dma((2,)),
             dma((8,)),
             dma((8,)),
             dma,
@@ -449,6 +459,16 @@
             collective_id=0, has_side_effects=True, vmem_limit_bytes=56 * 1024 * 1024
         ),
     )(mask_params, target, col_taps, row_taps, kernel_weights)
+    return pl.pallas_call(
+        functools.partial(finish, (expos, strips * cols)),
+        out_shape=(
+            jax.ShapeDtypeStruct(mask_params.shape, F32),
+            image,
+            jax.ShapeDtypeStruct((1,), F32),
+        ),
+        in_specs=[vmem] * 4,
+        out_specs=(vmem, vmem, smem),
+    )(mask_params, steps, resist, totals)
 
 
 def solution(mesh):

time: 35.5 us -> 32.4 us (0.913)
  local copies, waits for them, and re-layouts: 2.26 us -> 0 us
  between operations: 2.32 us -> 0.64 us
  Pallas kernels: 30.7 us -> 31.6 us
    unnamed x4 -> x0, local copies, waits for them, and re-layouts: 2.26 us -> none
    pallas_call x0 -> x1, Pallas kernels: none -> 1.82 us  [shards(): pl.pallas_call(functools.partial(finish, (expos, strips * cols)), out_sha...]
    pallas_call x1, Pallas kernels: 30.7 us -> 29.7 us  [shards(): pl.pallas_call(functools.partial(body, (strips, cols, expos, half)), out_...]
where the time goes in v5:
time: 32.4 us; the launch traced here: 32.2 us
  Pallas kernels  31.6 us (98%)
  between operations  0.64 us (2%)
    pallas_call x1, Pallas kernels, shards(): pl.pallas_call(functools.partial(body, (strips, cols, expos, half)), out_...  29.7 us
    pallas_call x1, Pallas kernels, shards(): pl.pallas_call(functools.partial(finish, (expos, strips * cols)), out_sha...  1.82 us

profile of v5, /device:TPU:0, one launch (start us, length us, event | category | flops | bytes accessed | tf_op | source)
XLA Modules:
  0.0 32.2 jit_solution(2214331198814283491)
XLA Ops:
  0.6 29.7 %shard_map.76 = (f32[256,128]{1,0:T(8,128)}, f32[256,128]{1,0:T(8,128)}, f32[8,128]{1,0:T(8,128)}) custom-call(f32[1,256,128]{2,1,0:T(8,128)} %params_ref.1, s32[256,128]{1,0:T(8,128)} %target_hbm.1, bf16[24,2,65]{2,1,0:T(2,128)(2,1)} %col_ref.1, bf16[24,2,65]{2,1,0:T(2,128)(2,1)} %row_ref.1, f32[24]{0:T(128)} %weight_ref.1), custom_call_target="tpu_custom_call" | custom-call | tf_op jit(solution)/shard_map/pallas_call | solution.py:422
  30.4 1.8 %shard_map.77 = (f32[1,256,128]{2,1,0:T(8,128)}, f32[256,128]{1,0:T(8,128)}, f32[1]{0:T(128)}) custom-call(f32[1,256,128]{2,1,0:T(8,128)} %params_ref.1, f32[256,128]{1,0:T(8,128)} %get-tuple-element.6.steps_ref, f32[256,128]{1,0:T(8,128)} %get-tuple-element.7.resist_in, f32[8,128]{1,0:T(8,128)} %get-tuple-element.8.totals_ref), custom_call_target="tpu_custom_call" | custom-call | tf_op jit(solution)/shard_map/pallas_call | solution.py:462

commit v6 on v5

--- a/solution.py
+++ b/solution.py
@@ -115,7 +115,7 @@
     target_now = target_ref[...].astype(F32)
     halo[1, two : two + width, tile : tile + rows] = target_now.T.astype(BF16)
 
-    def transfer(number):
+    def transfer(plane, number):
         down, right = DIRECTIONS[number]
         lane, lanes, to_lane = {
             -1: (tile, tile, tile + rows),
@@ -128,10 +128,10 @@
             1: (width, two, 0),
         }[right]
         return pltpu.make_async_remote_copy(
-            src_ref=halo.at[:, pl.ds(place, places), pl.ds(lane, lanes)],
-            dst_ref=halo.at[:, pl.ds(to_place, places), pl.ds(to_lane, lanes)],
-            send_sem=halo_send.at[number],
-            recv_sem=halo_recv.at[number],
+            src_ref=halo.at[plane, pl.ds(place, places), pl.ds(lane, lanes)],
+            dst_ref=halo.at[plane, pl.ds(to_place, places), pl.ds(to_lane, lanes)],
+            send_sem=halo_send.at[plane, number],
+            recv_sem=halo_recv.at[plane, number],
             device_id={
                 "strip": jnp.clip(strip + down, 0, strips - 1),
                 "col": jnp.clip(col + right, 0, cols - 1),
@@ -213,25 +213,29 @@
 
     pl.semaphore_wait(barrier, group - 1)
 
-    for number, (down, right) in enumerate(DIRECTIONS):
-
-        @pl.when(inside(down, right))
-        def _():
-            transfer(number).start()
+    for plane in range(2):
+        for number, (down, right) in enumerate(DIRECTIONS):
+
+            @pl.when(inside(down, right))
+            def _():
+                transfer(plane, number).start()
 
     lax.fori_loop(0, kernels, build_rows, 0)
     intensity[...] = jnp.zeros_like(intensity)
     descent[...] = jnp.zeros_like(descent)
 
-    for number, (down, right) in enumerate(DIRECTIONS):
-
-        @pl.when(inside(down, right))
-        def _():
-            transfer(number).wait_send()
-
-        @pl.when(inside(-down, -right))
-        def _():
-            transfer(number).wait_recv()
+    def receive(plane):
+        for number, (down, right) in enumerate(DIRECTIONS):
+
+            @pl.when(inside(down, right))
+            def _():
+                transfer(plane, number).wait_send()
+
+            @pl.when(inside(-down, -right))
+            def _():
+                transfer(plane, number).wait_recv()
+
+    receive(0)
 
     lanes = halo.shape[2]
     reach = rows + tile
@@ -278,7 +282,8 @@
     def row_passes(j, held):
         for i in range(batch):
             row_pass(j * batch + i, held.at[i])
-            build_adjoints(j * batch + i)
+            if i % 2 == 0:
+                build_adjoints(j * batch + i)
 
     def in_pairs(make, take, count, helds):
         make(0, helds[0])
@@ -307,6 +312,14 @@
         device_id_type=MESH,
     )
     swap.start()
+
+    def build_others(j, carry):
+        for i in range(1, batch, 2):
+            build_adjoints(j * batch + i)
+        return carry
+
+    lax.fori_loop(0, kernels // batch, build_others, 0)
+    receive(1)
     swap.wait()
 
     def side_by_side(ref):
@@ -352,17 +365,28 @@
         for band in range(bands):
             held[band] = returned[band * wide : (band + 1) * wide]
 
-    def gather(k, held):
-        found = [
-            jnp.concatenate(
-                [held[band, :, part * tile : (part + 1) * tile] for band in range(bands)], axis=1
-            )
-            for part in range(parts)
-        ]
-        source = jnp.concatenate([f[:tile] for f in found] + [f[tile:] for f in found], axis=0)
-        descent[...] += dot(col_adjoints[k], source)
-
-    in_pairs(correlate, gather, kernels, (even, odd))
+    def correlate_all(j, held):
+        for i in range(batch):
+            correlate(j * batch + i, held.at[i])
+
+    def gather_all(j, held):
+        sources = []
+        for i in range(batch):
+            found = [
+                jnp.concatenate(
+                    [
+                        held[i, band, :, part * tile : (part + 1) * tile]
+                        for band in range(bands)
+                    ],
+                    axis=1,
+                )
+                for part in range(parts)
+            ]
+            sources += [f[:tile] for f in found] + [f[tile:] for f in found]
+        matrix = jnp.concatenate([col_adjoints[j * batch + i] for i in range(batch)], axis=1)
+        descent[...] += dot(matrix, jnp.concatenate(sources, axis=0))
+
+    in_pairs(correlate_all, gather_all, kernels // batch, (even, odd))
 
     mask = jax.nn.sigmoid(mask_slope * params_ref[0])
     gradient = descent[...].T * mask_slope * mask * (1.0 - mask)
@@ -394,15 +418,19 @@
     totals_ref[...] = jnp.sum(slots[...], axis=0)
 
 
-def finish(copies, params_ref, steps_ref, resist_in, totals_ref, new_ref, resist_ref, loss_ref):
+def finish(
+    copies, params_ref, steps_ref, resist_in, totals_ref, new_ref, resist_ref, loss_ref, sem
+):
+    passing = pltpu.make_async_copy(resist_in, resist_ref, sem)
+    passing.start()
     expos, blocks = copies
-    rows, width = resist_in.shape
+    rows, width = steps_ref.shape
     pixels = rows * width * blocks
     loss_ref[0] = jnp.sum(totals_ref[0:1, :]) / (expos * pixels)
     square_sum = jnp.sum(totals_ref[1:2, :], axis=1, keepdims=True)
     root_mean = jnp.sqrt(square_sum / (expos * pixels) + norm_eps)
     new_ref[0] = params_ref[0] - step_length * steps_ref[...] / root_mean
-    resist_ref[...] = resist_in[...]
+    passing.wait()
 
 
 def shards(mask_params, target, col_taps, row_taps, kernel_weights):
@@ -442,14 +470,14 @@
             pltpu.VMEM((bands + 1, wide, tile), F32),
             pltpu.VMEM((bands + 1, wide, tile), F32),
             pltpu.VMEM((bands + 1, wide, tile), F32),
-            pltpu.VMEM((bands, wide, 2 * tile), BF16),
-            pltpu.VMEM((bands, wide, 2 * tile), BF16),
+            pltpu.VMEM((batch, bands, wide, 2 * tile), BF16),
+            pltpu.VMEM((batch, bands, wide, 2 * tile), BF16),
             pltpu.VMEM((width, rows), F32),
             pltpu.VMEM((8, width), F32),
             pltpu.VMEM((group, 8, width), F32),
             dma((2,)),
-            dma((8,)),
-            dma((8,)),
+            dma((2, 8)),
+            dma((2, 8)),
             dma,
             dma,
             dma((group,)),
@@ -466,8 +494,9 @@
             image,
             jax.ShapeDtypeStruct((1,), F32),
         ),
-        in_specs=[vmem] * 4,
-        out_specs=(vmem, vmem, smem),
+        in_specs=[vmem, vmem, anywhere, vmem],
+        out_specs=(vmem, anywhere, smem),
+        scratch_shapes=[dma],
     )(mask_params, steps, resist, totals)
 
 

time: 32.4 us -> 35.8 us (1.10)
  Pallas kernels: 31.6 us -> 34.9 us
    pallas_call x1, Pallas kernels: 1.82 us -> 6.71 us  [shards(): pl.pallas_call(functools.partial(finish, (expos, strips * cols)), out_sha...]
    pallas_call x1, Pallas kernels: 29.7 us -> 28.2 us  [shards(): pl.pallas_call(functools.partial(body, (strips, cols, expos, half)), out_...]
where the time goes in v6:
time: 35.8 us; the launch traced here: 35.5 us
  Pallas kernels  34.9 us (97%)
  between operations  0.64 us (2%)
    pallas_call x1, Pallas kernels, shards(): pl.pallas_call(functools.partial(body, (strips, cols, expos, half)), out_...  28.2 us
    pallas_call x1, Pallas kernels, shards(): pl.pallas_call(functools.partial(finish, (expos, strips * cols)), out_sha...  6.71 us

profile of v6, /device:TPU:0, one launch (start us, length us, event | category | flops | bytes accessed | tf_op | source)
XLA Modules:
  0.0 35.5 jit_solution(4154923391205014831)
XLA Ops:
  0.6 28.2 %shard_map.76 = (f32[256,128]{1,0:T(8,128)}, f32[256,128]{1,0:T(8,128)}, f32[8,128]{1,0:T(8,128)}) custom-call(f32[1,256,128]{2,1,0:T(8,128)} %params_ref.1, s32[256,128]{1,0:T(8,128)} %target_hbm.1, bf16[24,2,65]{2,1,0:T(2,128)(2,1)} %col_ref.1, bf16[24,2,65]{2,1,0:T(2,128)(2,1)} %row_ref.1, f32[24]{0:T(128)} %weight_ref.1), custom_call_target="tpu_custom_call" | custom-call | tf_op jit(solution)/shard_map/pallas_call | solution.py:450
  28.8 6.7 %shard_map.77 = (f32[1,256,128]{2,1,0:T(8,128)}, f32[256,128]{1,0:T(8,128)}, f32[1]{0:T(128)}) custom-call(f32[1,256,128]{2,1,0:T(8,128)} %params_ref.1, f32[256,128]{1,0:T(8,128)} %get-tuple-element.6.steps_ref, f32[256,128]{1,0:T(8,128)} %get-tuple-element.7.resist_in, f32[8,128]{1,0:T(8,128)} %get-tuple-element.8.totals_ref), custom_call_target="tpu_custom_call" | custom-call | tf_op jit(solution)/shard_map/pallas_call | solution.py:490

commit v7 on v6

--- a/solution.py
+++ b/solution.py
@@ -27,14 +27,17 @@
     sizes,
     params_hbm,
     target_hbm,
-    col_ref,
-    row_ref,
-    weight_ref,
+    col_hbm,
+    row_hbm,
+    weight_hbm,
     steps_ref,
     resist_ref,
     totals_ref,
     params_ref,
     target_ref,
+    col_ref,
+    row_ref,
+    weight_ref,
     halo,
     windows,
     padded,
@@ -53,6 +56,7 @@
     even,
     odd,
     descent,
+    shown,
     partial,
     slots,
     fetch_sem,
@@ -95,7 +99,13 @@
     fetches = [
         pltpu.make_async_copy(source, into, fetch_sem.at[number])
         for number, (source, into) in enumerate(
-            ((params_hbm, params_ref), (target_hbm, target_ref))
+            (
+                (params_hbm, params_ref),
+                (target_hbm, target_ref),
+                (col_hbm, col_ref),
+                (row_hbm, row_ref),
+                (weight_hbm, weight_ref),
+            )
         )
     ]
     for fetch in fetches:
@@ -108,7 +118,7 @@
     for place, _ in peers:
         pl.semaphore_signal(barrier, inc=1, device_id=place, device_id_type=MESH)
 
-    for fetch in fetches:
+    for fetch in fetches[:2]:
         fetch.wait()
     mask = jax.nn.sigmoid(mask_slope * params_ref[0])
     halo[0, two : two + width, tile : tile + rows] = mask.T.astype(BF16)
@@ -143,6 +153,17 @@
         to_strip, to_col = (strip + down, col + right)
         return (to_strip >= 0) & (to_strip < strips) & (to_col >= 0) & (to_col < cols)
 
+    pl.semaphore_wait(barrier, group - 1)
+
+    for plane in range(2):
+        for number, (down, right) in enumerate(DIRECTIONS):
+
+            @pl.when(inside(down, right))
+            def _():
+                transfer(plane, number).start()
+
+    for fetch in fetches[2:]:
+        fetch.wait()
     padded[...] = jnp.zeros_like(padded)
     for k in range(kernels):
         for table, source in enumerate((col_ref, row_ref)):
@@ -210,15 +231,6 @@
         )
 
     lax.fori_loop(0, kernels, build_cols, 0)
-
-    pl.semaphore_wait(barrier, group - 1)
-
-    for plane in range(2):
-        for number, (down, right) in enumerate(DIRECTIONS):
-
-            @pl.when(inside(down, right))
-            def _():
-                transfer(plane, number).start()
 
     lax.fori_loop(0, kernels, build_rows, 0)
     intensity[...] = jnp.zeros_like(intensity)
@@ -289,17 +301,23 @@
         make(0, helds[0])
         size = next(size for size in (4, 2, 1) if count % size == 0)
 
-        def step(j, carry):
+        def step(j, final):
             for i in range(size):
                 k = size * j + i
+                ahead = not (final and i == size - 1)
                 if size == 1:
                     take(k, helds[0])
-                make(jnp.minimum(k + 1, count - 1), helds[(i + 1) % 2 if size > 1 else 0])
+                if ahead:
+                    make(k + 1, helds[(i + 1) % 2 if size > 1 else 0])
                 if size > 1:
                     take(k, helds[i % 2])
+
+        def looped(j, carry):
+            step(j, False)
             return carry
 
-        lax.fori_loop(0, count // size, step, 0)
+        lax.fori_loop(0, count // size - 1, looped, 0)
+        step(count // size - 1, True)
 
     in_pairs(col_pass, row_passes, kernels // batch, (even_columns, odd_columns))
 
@@ -344,10 +362,15 @@
     steepness = jnp.where(kept, 2.0 * mismatch * resist_steep * resist * (1.0 - resist), 0.0)
     for band in range(bands + 1):
         slope[band] = steepness[:, band * tile : (band + 1) * tile]
-    own = pltpu.roll(resist[half : half + width, :], reach - half, 1)[:, :rows].T
-    resist_ref[...] = own
-    own_miss = own - target_ref[...].astype(F32)
-    loss_line = jnp.sum(own_miss * own_miss, axis=0, keepdims=True)
+    owned = (
+        (row_lanes >= half)
+        & (row_lanes < half + rows)
+        & (col_ids >= col * width)
+        & (col_ids < (col + 1) * width)
+    )
+    missed = jnp.sum(jnp.where(owned, mismatch * mismatch, 0.0), axis=0, keepdims=True)
+    loss_line = sum(missed[:, band * tile : (band + 1) * tile] for band in range(bands + 1))
+    shown[...] = resist[half : half + width, :]
 
     def correlate(k, held):
         scale = 2.0 * weight_ref[k]
@@ -412,17 +435,15 @@
             )
     for share in shares:
         share.start()
+    resist_ref[...] = pltpu.roll(shown[...], reach - half, 1)[:, :rows].T
+
     for arrival in arrivals:
         arrival.wait()
 
     totals_ref[...] = jnp.sum(slots[...], axis=0)
 
 
-def finish(
-    copies, params_ref, steps_ref, resist_in, totals_ref, new_ref, resist_ref, loss_ref, sem
-):
-    passing = pltpu.make_async_copy(resist_in, resist_ref, sem)
-    passing.start()
+def finish(copies, params_ref, steps_ref, resist_in, totals_ref, new_ref, resist_ref, loss_ref):
     expos, blocks = copies
     rows, width = steps_ref.shape
     pixels = rows * width * blocks
@@ -430,7 +451,7 @@
     square_sum = jnp.sum(totals_ref[1:2, :], axis=1, keepdims=True)
     root_mean = jnp.sqrt(square_sum / (expos * pixels) + norm_eps)
     new_ref[0] = params_ref[0] - step_length * steps_ref[...] / root_mean
-    passing.wait()
+    resist_ref[...] = resist_in[...]
 
 
 def shards(mask_params, target, col_taps, row_taps, kernel_weights):
@@ -446,15 +467,18 @@
     dma = pltpu.SemaphoreType.DMA
     image = jax.ShapeDtypeStruct(target.shape, F32)
     batch = next(size for size in (4, 3, 2, 1) if kernels % size == 0)
-    anywhere = pl.BlockSpec(memory_space=pl.ANY)
+    anywhere = pl.BlockSpec(memory_space=pltpu.HBM)
     steps, resist, totals = pl.pallas_call(
         functools.partial(body, (strips, cols, expos, half)),
         out_shape=(image, image, jax.ShapeDtypeStruct((8, width), F32)),
-        in_specs=[anywhere, anywhere, vmem, vmem, smem],
+        in_specs=[anywhere] * 5,
         out_specs=(vmem, vmem, vmem),
         scratch_shapes=[
             pltpu.VMEM(mask_params.shape, F32),
             pltpu.VMEM(target.shape, target.dtype),
+            pltpu.VMEM(col_taps.shape, col_taps.dtype),
+            pltpu.VMEM(row_taps.shape, row_taps.dtype),
+            pltpu.SMEM(kernel_weights.shape, F32),
             pltpu.VMEM((2, width + 2 * two, rows + 2 * tile), BF16),
             pltpu.VMEM((tile, (wide // two) * (rows + tile)), BF16),
             pltpu.VMEM((2, 2 * kernels, tile), F32),
@@ -473,9 +497,10 @@
             pltpu.VMEM((batch, bands, wide, 2 * tile), BF16),
             pltpu.VMEM((batch, bands, wide, 2 * tile), BF16),
             pltpu.VMEM((width, rows), F32),
+            pltpu.VMEM((width, rows + tile), F32),
             pltpu.VMEM((8, width), F32),
             pltpu.VMEM((group, 8, width), F32),
-            dma((2,)),
+            dma((5,)),
             dma((2, 8)),
             dma((2, 8)),
             dma,
@@ -484,7 +509,7 @@
             dma((group,)),
         ],
         compiler_params=pltpu.CompilerParams(
-            collective_id=0, has_side_effects=True, vmem_limit_bytes=56 * 1024 * 1024
+            collective_id=0, has_side_effects=True, vmem_limit_bytes=40 * 1024 * 1024
         ),
     )(mask_params, target, col_taps, row_taps, kernel_weights)
     return pl.pallas_call(
@@ -494,9 +519,8 @@
             image,
             jax.ShapeDtypeStruct((1,), F32),
         ),
-        in_specs=[vmem, vmem, anywhere, vmem],
-        out_specs=(vmem, anywhere, smem),
-        scratch_shapes=[dma],
+        in_specs=[vmem] * 4,
+        out_specs=(vmem, vmem, smem),
     )(mask_params, steps, resist, totals)
 
 

time: 35.8 us -> 34.6 us (0.966)
  Pallas kernels: 34.9 us -> 27.8 us
  local copies, waits for them, and re-layouts: 0 us -> 5.75 us
    unnamed x0 -> x16, local copies, waits for them, and re-layouts: none -> 5.75 us
    pallas_call x1, Pallas kernels: 6.71 us -> 1.81 us  [shards(): pl.pallas_call(functools.partial(finish, (expos, strips * cols)), out_sha...]
    pallas_call x1, Pallas kernels: 28.2 us -> 26 us  [shards(): pl.pallas_call(functools.partial(body, (strips, cols, expos, half)), out_...]
where the time goes in v7:
time: 34.6 us; the launch traced here: 34.3 us
  Pallas kernels  27.8 us (80%)
  local copies, waits for them, and re-layouts  5.75 us (17%)
  between operations  0.66 us (2%)
    pallas_call x1, Pallas kernels, shards(): pl.pallas_call(functools.partial(body, (strips, cols, expos, half)), out_...  26 us
    unnamed x16, local copies, waits for them, and re-layouts  5.75 us
    pallas_call x1, Pallas kernels, shards(): pl.pallas_call(functools.partial(finish, (expos, strips * cols)), out_sha...  1.81 us

profile of v7, /device:TPU:0, one launch (start us, length us, event | category | flops | bytes accessed | tf_op | source)
XLA Modules:
  0.0 34.3 jit_solution(4682728715985932126)
XLA Ops:
  0.6 0.0 copy-start
  0.6 0.9 %copy-done = f32[1,256,128]{2,1,0:T(8,128)S(1)} copy-done((f32[1,256,128]{2,1,0:T(8,128)S(1)}, f32[1,256,128]{2,1,0:T(8,128)}, u32[]{:S(2)}) %copy-start) | copy-done | bytes 131096
  1.5 0.0 copy-start.3
  1.5 0.9 %copy-done.3 = s32[256,128]{1,0:T(8,128)S(1)} copy-done((s32[256,128]{1,0:T(8,128)S(1)}, s32[256,128]{1,0:T(8,128)}, u32[]{:S(2)}) %copy-start.3) | copy-done | bytes 131096
  2.4 0.0 copy-start.4
  2.4 0.7 %copy-done.4 = bf16[24,2,65]{2,1,0:T(2,128)(2,1)S(1)} copy-done((bf16[24,2,65]{2,1,0:T(2,128)(2,1)S(1)}, bf16[24,2,65]{2,1,0:T(2,128)(2,1)}, u32[]{:S(2)}) %copy-start.4) | copy-done | bytes 6264
  3.2 0.0 copy-start.5
  3.2 0.7 %copy-done.5 = bf16[24,2,65]{2,1,0:T(2,128)(2,1)S(1)} copy-done((bf16[24,2,65]{2,1,0:T(2,128)(2,1)S(1)}, bf16[24,2,65]{2,1,0:T(2,128)(2,1)}, u32[]{:S(2)}) %copy-start.5) | copy-done | bytes 6264
  3.9 0.0 copy-start.7
  3.9 0.7 %copy-done.7 = f32[24]{0:T(128)S(1)} copy-done((f32[24]{0:T(128)S(1)}, f32[24]{0:T(128)}, u32[]{:S(2)}) %copy-start.7) | copy-done | bytes 120
  4.5 26.0 %shard_map.76 = (f32[256,128]{1,0:T(8,128)S(1)}, f32[256,128]{1,0:T(8,128)S(1)}, f32[8,128]{1,0:T(8,128)S(1)}) custom-call(f32[1,256,128]{2,1,0:T(8,128)S(1)} %copy-done, s32[256,128]{1,0:T(8,128)S(1)} %copy-done.3, bf16[24,2,65]{2,1,0:T(2,128)(2,1)S(1)} %copy-done.4, bf16[24,2,65]{2,1,0:T(2,128)(2,1)S(1)} %copy-done.5, f32[24]{0:T(128)S(1)} %copy-done.7), custom_call_target="tpu_custom_call" | custom-call | tf_op jit(solution)/shard_map/pallas_call | solution.py:471
  30.6 0.0 copy-start.1
  30.6 0.6 %copy-done.1 = f32[256,128]{1,0:T(8,128)} copy-done((f32[256,128]{1,0:T(8,128)}, f32[256,128]{1,0:T(8,128)S(1)}, u32[]{:S(2)}) %copy-start.1) | copy-done | bytes 131096
  31.2 0.0 copy-start.2
  31.2 0.7 %copy-done.2 = f32[256,128]{1,0:T(8,128)} copy-done((f32[256,128]{1,0:T(8,128)}, f32[256,128]{1,0:T(8,128)S(1)}, u32[]{:S(2)}) %copy-start.2) | copy-done | bytes 131096
  31.9 0.0 copy-start.6
  31.9 0.6 %copy-done.6 = f32[8,128]{1,0:T(8,128)} copy-done((f32[8,128]{1,0:T(8,128)}, f32[8,128]{1,0:T(8,128)S(1)}, u32[]{:S(2)}) %copy-start.6) | copy-done | bytes 4120
  32.4 1.8 %shard_map.77 = (f32[1,256,128]{2,1,0:T(8,128)}, f32[256,128]{1,0:T(8,128)}, f32[1]{0:T(128)}) custom-call(f32[1,256,128]{2,1,0:T(8,128)} %params_ref.1, f32[256,128]{1,0:T(8,128)} %copy-done.1, f32[256,128]{1,0:T(8,128)} %copy-done.2, f32[8,128]{1,0:T(8,128)} %copy-done.6), custom_call_target="tpu_custom_call" | custom-call | tf_op jit(solution)/shard_map/pallas_call | solution.py:515
Async XLA Ops:
  0.6 0.9 %copy-start = (f32[1,256,128]{2,1,0:T(8,128)S(1)}, f32[1,256,128]{2,1,0:T(8,128)}, u32[]{:S(2)}) copy-start(f32[1,256,128]{2,1,0:T(8,128)} %params_ref.1) | copy-start | bytes 393220
  1.5 0.9 %copy-start.3 = (s32[256,128]{1,0:T(8,128)S(1)}, s32[256,128]{1,0:T(8,128)}, u32[]{:S(2)}) copy-start(s32[256,128]{1,0:T(8,128)} %target_hbm.1) | copy-start | bytes 393220
  2.4 0.7 %copy-start.4 = (bf16[24,2,65]{2,1,0:T(2,128)(2,1)S(1)}, bf16[24,2,65]{2,1,0:T(2,128)(2,1)}, u32[]{:S(2)}) copy-start(bf16[24,2,65]{2,1,0:T(2,128)(2,1)} %col_hbm.1) | copy-start | bytes 18724
  3.2 0.7 %copy-start.5 = (bf16[24,2,65]{2,1,0:T(2,128)(2,1)S(1)}, bf16[24,2,65]{2,1,0:T(2,128)(2,1)}, u32[]{:S(2)}) copy-start(bf16[24,2,65]{2,1,0:T(2,128)(2,1)} %row_hbm.1) | copy-start | bytes 18724
  3.9 0.7 %copy-start.7 = (f32[24]{0:T(128)S(1)}, f32[24]{0:T(128)}, u32[]{:S(2)}) copy-start(f32[24]{0:T(128)} %weight_hbm.1) | copy-start | bytes 292
  30.6 0.7 %copy-start.1 = (f32[256,128]{1,0:T(8,128)}, f32[256,128]{1,0:T(8,128)S(1)}, u32[]{:S(2)}) copy-start(f32[256,128]{1,0:T(8,128)S(1)} %get-tuple-element.6.steps_ref) | copy-start | bytes 393220
  31.2 0.7 %copy-start.2 = (f32[256,128]{1,0:T(8,128)}, f32[256,128]{1,0:T(8,128)S(1)}, u32[]{:S(2)}) copy-start(f32[256,128]{1,0:T(8,128)S(1)} %get-tuple-element.7.resist_in) | copy-start | bytes 393220
  31.9 0.6 %copy-start.6 = (f32[8,128]{1,0:T(8,128)}, f32[8,128]{1,0:T(8,128)S(1)}, u32[]{:S(2)}) copy-start(f32[8,128]{1,0:T(8,128)S(1)} %get-tuple-element.8.totals_ref) | copy-start | bytes 12292

commit v8 on v7

--- a/solution.py
+++ b/solution.py
@@ -509,7 +509,7 @@
             dma((group,)),
         ],
         compiler_params=pltpu.CompilerParams(
-            collective_id=0, has_side_effects=True, vmem_limit_bytes=40 * 1024 * 1024
+            collective_id=0, has_side_effects=True, vmem_limit_bytes=56 * 1024 * 1024
         ),
     )(mask_params, target, col_taps, row_taps, kernel_weights)
     return pl.pallas_call(

time: 34.6 us -> 29.2 us (0.84)
  local copies, waits for them, and re-layouts: 5.75 us -> 0 us
  Pallas kernels: 27.8 us -> 28.4 us
    unnamed x16 -> x0, local copies, waits for them, and re-layouts: 5.75 us -> none
    pallas_call x1, Pallas kernels: 26 us -> 26.6 us  [shards(): pl.pallas_call(functools.partial(body, (strips, cols, expos, half)), out_...]
where the time goes in v8:
time: 29.2 us; the launch traced here: 29.1 us
  Pallas kernels  28.4 us (97%)
  between operations  0.64 us (2%)
    pallas_call x1, Pallas kernels, shards(): pl.pallas_call(functools.partial(body, (strips, cols, expos, half)), out_...  26.6 us
    pallas_call x1, Pallas kernels, shards(): pl.pallas_call(functools.partial(finish, (expos, strips * cols)), out_sha...  1.82 us

profile of v8, /device:TPU:0, one launch (start us, length us, event | category | flops | bytes accessed | tf_op | source)
XLA Modules:
  0.0 29.1 jit_solution(4784398615882107511)
XLA Ops:
  0.6 26.6 %shard_map.76 = (f32[256,128]{1,0:T(8,128)}, f32[256,128]{1,0:T(8,128)}, f32[8,128]{1,0:T(8,128)}) custom-call(f32[1,256,128]{2,1,0:T(8,128)} %params_ref.1, s32[256,128]{1,0:T(8,128)} %target_hbm.1, bf16[24,2,65]{2,1,0:T(2,128)(2,1)} %col_hbm.1, bf16[24,2,65]{2,1,0:T(2,128)(2,1)} %row_hbm.1, f32[24]{0:T(128)} %weight_hbm.1), custom_call_target="tpu_custom_call" | custom-call | tf_op jit(solution)/shard_map/pallas_call | solution.py:471
  27.2 1.8 %shard_map.77 = (f32[1,256,128]{2,1,0:T(8,128)}, f32[256,128]{1,0:T(8,128)}, f32[1]{0:T(128)}) custom-call(f32[1,256,128]{2,1,0:T(8,128)} %params_ref.1, f32[256,128]{1,0:T(8,128)} %get-tuple-element.6.steps_ref, f32[256,128]{1,0:T(8,128)} %get-tuple-element.7.resist_in, f32[8,128]{1,0:T(8,128)} %get-tuple-element.8.totals_ref), custom_call_target="tpu_custom_call" | custom-call | tf_op jit(solution)/shard_map/pallas_call | solution.py:515
